TPU v7x, 32 devices: a whole 2x2x4 slice. The times are simulated.
32 devices in a mesh: rollout: 4 (over z), branch: 2 (over x), tensor: 4 (over y, core).
Axes of the slice: x: 2, y: 2, z: 4, core: 2. Of those that a mesh axis runs over, the one named last changes fastest.
Arguments:
- tokens: bfloat16 [8192, 2048], P(('rollout', 'branch')), parts along dimension 0, as said below
- parents: int32 [32], P('rollout'), parts along dimension 0, may hold values from 0 to 6, as said below
- lengths: int32 [32], P('rollout'), parts along dimension 0, may hold values from 128 to 256, as said below
- lin_qkv: bfloat16 [2048, 3, 1024], P(None, None, 'tensor'), may hold values from -0.125 to 0.125
- lin_gates: bfloat16 [2048, 2, 8], P(None, None, 'tensor'), as said below
- decay_rate: float32 [8], P('tensor'), as said below
- lin_out: bfloat16 [1024, 2048], P('tensor'), may hold values from -4 to 4
- norm_gain: float32 [2048], replicated, may hold values from 0.1 to 1.9
- att_q: bfloat16 [2048, 2048], P(None, 'tensor'), as said below
- att_kv: bfloat16 [2048, 2, 512], replicated, as said below
Outputs:
- lin_mixed: bfloat16 [8192, 2048], P(('rollout', 'branch', 'tensor')), parts along dimension 0
- att_out: bfloat16 [8192, 2048], P(('rollout', 'branch'), 'tensor'), parts along dimension 0
There are 4 independent parts, one for each index of `rollout`. A program takes and returns all parts, laid end to end along the dimension named above; an argument that names none is the same for every part. Nothing has to cross between parts.
Inputs may be any that keep to these rules, and one draw needn't show every extreme that they name: parents[0] = 0 marks the root; every other branch's parent is an earlier branch; the last branch's parent is the branch just before it. `lengths`: a multiple of 128; some branch has 256 valid tokens and some has 128. `decay_rate`: positive. `tokens`: entries of order one. `lin_gates`: entries of order one over the square root of 2048. `att_q`: entries of order one over the square root of 2048. `att_kv`: entries of order one over the square root of 2048.
All inputs are finite; a program needn't handle non-finite values.
Results may differ from a plain program's by a relative error of at most 0.035.
Values may be sent and summed in bfloat16 or wider, within the bound.
A program may use at most 128 MiB of HBM per device.

v0:
```python
import math

import jax
import jax.numpy as jnp
from jax import lax
from jax.sharding import PartitionSpec as P

KV_HEADS = 2
ATT_DIM = 256
BLOCK = 64
SEG = 256


highest = lax.Precision.HIGHEST


def unit_rows(matrix):
    return matrix * lax.rsqrt(jnp.sum(matrix * matrix, axis=-1, keepdims=True) + 1e-06)


def ancestor_table(parent_map):
    count = parent_map.shape[0]

    def widen(counter, table):
        return parent_map + jnp.dot(parent_map, table, precision=highest)

    return lax.fori_loop(0, count - 1, widen, parent_map)


def block_terms(q_unit, k_unit, values, beta, log_decay):
    blocks = q_unit.shape[0] // BLOCK

    def split_block(array):
        shaped = array.reshape((blocks, BLOCK) + array.shape[1:])
        return jnp.swapaxes(shaped, 1, 2)

    queries = split_block(q_unit)
    keys_blk = split_block(k_unit)
    vals_blk = split_block(values)
    beta_blk = split_block(beta)
    decay_blk = jnp.cumsum(split_block(log_decay), axis=-1)
    final_decay = decay_blk[..., -1:]
    gap = decay_blk[..., :, None] - decay_blk[..., None, :]
    places = jnp.arange(BLOCK)
    strict = places[:, None] > places[None, :]
    inclusive = places[:, None] >= places[None, :]
    key_key = jnp.einsum("nhtd,nhsd->nhts", keys_blk, keys_blk, precision=highest)
    query_key = jnp.einsum("nhtd,nhsd->nhts", queries, keys_blk, precision=highest)
    lower_part = jnp.where(
        strict, beta_blk[..., :, None] * jnp.exp(jnp.where(strict, gap, 0.0)) * key_key, 0.0
    )
    system = lower_part + jnp.eye(BLOCK, dtype=lower_part.dtype)
    right_hand = jnp.concatenate(
        [beta_blk[..., None] * vals_blk, (beta_blk * jnp.exp(decay_blk))[..., None] * keys_blk],
        axis=-1,
    )
    solved = jax.scipy.linalg.solve_triangular(system, right_hand, lower=True, unit_diagonal=True)
    value_width = vals_blk.shape[-1]
    pseudo = solved[..., :value_width]
    weighted = solved[..., value_width:]
    carried_keys = jnp.exp(final_decay - decay_blk)[..., None] * keys_blk
    scaled_queries = jnp.exp(decay_blk)[..., None] * queries
    mixing = jnp.where(inclusive, jnp.exp(jnp.where(inclusive, gap, 0.0)) * query_key, 0.0)
    overall = jnp.exp(final_decay[..., 0])
    return (pseudo, weighted, carried_keys, scaled_queries, mixing, overall)


def run_outputs(initial, terms):

    def run_advance(current, block_part):
        pseudo, weighted, carried_keys, scaled_queries, mixing, overall = block_part
        update = pseudo - jnp.einsum("htk,hkm->htm", weighted, current, precision=highest)
        produced = jnp.einsum("htk,hkm->htm", scaled_queries, current, precision=highest)
        produced = produced + jnp.einsum("hts,hsm->htm", mixing, update, precision=highest)
        renewed = overall[:, None, None] * current + jnp.einsum(
            "htk,htm->hkm", carried_keys, update, precision=highest
        )
        return (renewed, produced)

    final_state, produced = lax.scan(run_advance, initial, terms)
    blocks, head_count, block_len, value_width = produced.shape
    return (
        final_state,
        jnp.swapaxes(produced, 1, 2).reshape(blocks * block_len, head_count, value_width),
    )


def affine_map(terms):
    pseudo, weighted, carried_keys, scaled_queries, mixing, overall = terms
    head_count = pseudo.shape[1]
    key_width = weighted.shape[-1]
    value_width = pseudo.shape[-1]
    extended = jnp.concatenate([pseudo, jnp.zeros(weighted.shape, jnp.float32)], axis=-1)
    identity = jnp.broadcast_to(
        jnp.eye(key_width, dtype=jnp.float32), (head_count, key_width, key_width)
    )
    initial = jnp.concatenate(
        [jnp.zeros((head_count, key_width, value_width), jnp.float32), identity], axis=-1
    )

    def affine_advance(current, block_part):
        pseudo_ext, weighted_blk, keys_blk, overall_blk = block_part
        update = pseudo_ext - jnp.einsum("htk,hkm->htm", weighted_blk, current, precision=highest)
        renewed = overall_blk[:, None, None] * current + jnp.einsum(
            "htk,htm->hkm", keys_blk, update, precision=highest
        )
        return (renewed, None)

    final_state, unused = lax.scan(
        affine_advance, initial, (extended, weighted, carried_keys, overall)
    )
    return (final_state[..., :value_width], final_state[..., value_width:])


def normalize(mixed, norm_gain):
    scaled = mixed * lax.rsqrt(jnp.mean(mixed * mixed, axis=-1, keepdims=True) + 1e-06) * norm_gain
    return scaled.astype(jnp.bfloat16)


def on_device(
    tokens, parents, lengths, lin_qkv, lin_gates, decay_rate, lin_out, norm_gain, att_q, att_kv
):
    branch_idx = lax.axis_index("branch")
    tensor_count = lax.axis_size("tensor")
    tensor_idx = lax.axis_index("tensor")
    local_rows = tokens.shape[0]
    local_count = local_rows // SEG
    segment_count = lax.axis_size("branch") * local_count
    model_width = tokens.shape[1]
    local_heads = decay_rate.shape[0]
    head_dim = lin_qkv.shape[2] // local_heads
    att_dim = ATT_DIM
    seg_ids = jnp.arange(segment_count)
    first_seg = branch_idx * local_count
    local_segs = first_seg + jnp.arange(local_count)
    local_flag = seg_ids[None, :] == local_segs[:, None]
    own_lengths = jnp.sum(jnp.where(local_flag, lengths[None, :], 0), axis=1)
    seg_positions = jnp.arange(SEG)
    valid = (seg_positions[None, :] < own_lengths[:, None]).reshape(local_rows)
    row_local = jnp.arange(local_rows)
    query_seg = first_seg + row_local // SEG
    query_pos = row_local % SEG
    projected = jnp.dot(
        tokens, lin_qkv.reshape(model_width, -1), preferred_element_type=jnp.float32
    )
    projected = projected.reshape(local_rows, 3, local_heads, head_dim)
    q_unit = unit_rows(projected[:, 0]) / math.sqrt(head_dim)
    k_unit = unit_rows(projected[:, 1])
    values = projected[:, 2]
    gate_raw = jnp.dot(
        tokens, lin_gates.reshape(model_width, -1), preferred_element_type=jnp.float32
    )
    gate_raw = gate_raw.reshape(local_rows, 2, local_heads)
    beta = jnp.where(valid[:, None], jax.nn.sigmoid(gate_raw[:, 1]), 0.0)
    log_decay = jnp.where(
        valid[:, None], -decay_rate[None, :] * jax.nn.softplus(gate_raw[:, 0]), 0.0
    )

    def split_branches(array):
        return array.reshape((local_count, SEG) + array.shape[1:])

    terms = jax.vmap(block_terms)(
        split_branches(q_unit),
        split_branches(k_unit),
        split_branches(values),
        split_branches(beta),
        split_branches(log_decay),
    )
    own_offset, own_linear = jax.vmap(affine_map)(terms)
    parent_map = ((parents[:, None] == seg_ids[None, :]) & (seg_ids[:, None] > 0)).astype(
        jnp.float32
    )
    local_onehot = local_flag.astype(jnp.float32)
    ancestry = ancestor_table(parent_map)
    local_anc = (jnp.dot(local_onehot, ancestry, precision=highest) > 0.5).astype(jnp.float32)
    all_offsets, all_linear = (
        lax.all_gather(own_offset, "branch", axis=0, tiled=True),
        lax.all_gather(own_linear, "branch", axis=0, tiled=True),
    )

    def replay(counter, starts):
        ends = jnp.einsum("nhij,nhjv->nhiv", all_linear, starts, precision=highest) + all_offsets
        return jnp.einsum("ji,ihdv->jhdv", parent_map, ends, precision=highest)

    starts = lax.fori_loop(0, segment_count - 1, replay, jnp.zeros(all_offsets.shape, jnp.float32))
    own_start = lax.dynamic_slice_in_dim(starts, first_seg, local_count, 0)
    final_state, lin_heads = jax.vmap(run_outputs)(own_start, terms)
    lin_values = jnp.where(valid[:, None], lin_heads.reshape(local_rows, -1), 0.0).astype(
        jnp.bfloat16
    )
    partial_sum = jnp.dot(lin_values, lin_out, preferred_element_type=jnp.float32)
    local_q = att_q.shape[1] // att_dim
    kv_head = tensor_idx // (tensor_count // KV_HEADS)
    scale_factor = 1.0 / math.sqrt(att_dim)
    query_anc = jnp.repeat(local_anc, SEG, axis=0)
    quarter = local_rows // tensor_count
    summed = lax.psum_scatter(partial_sum, "tensor", scatter_dimension=0, tiled=True)
    own_rows = lax.dynamic_slice_in_dim(tokens, tensor_idx * quarter, quarter, 0)
    mixed_rows = summed + own_rows.astype(jnp.float32)
    lin_mixed = mixed_rows.astype(jnp.bfloat16)
    normed_rows = normalize(mixed_rows, norm_gain)
    kv_rows = jnp.dot(
        normed_rows, att_kv.reshape(model_width, -1), preferred_element_type=jnp.float32
    ).astype(jnp.bfloat16)
    half_cols = kv_rows.shape[1] // 2
    normed_full = lax.all_gather(normed_rows, "tensor", axis=0, tiled=True)
    queries = jnp.dot(normed_full, att_q, preferred_element_type=jnp.float32).astype(jnp.bfloat16)
    queries = queries.reshape(local_rows, local_q, att_dim)
    key_part = lax.dynamic_slice_in_dim(
        lax.all_gather(kv_rows[:, :half_cols], ("branch", "tensor"), axis=0, tiled=True),
        kv_head * att_dim,
        att_dim,
        1,
    )
    value_part = lax.dynamic_slice_in_dim(
        lax.all_gather(kv_rows[:, half_cols:], ("branch", "tensor"), axis=0, tiled=True),
        kv_head * att_dim,
        att_dim,
        1,
    )
    global_rows = jnp.arange(key_part.shape[0])
    key_seg = global_rows // SEG
    key_pos = global_rows % SEG
    match = key_seg[:, None] == seg_ids[None, :]
    key_limit = jnp.sum(jnp.where(match, lengths[None, :], 0), axis=1)
    key_ancestor = jnp.dot(query_anc, match.astype(jnp.float32).T, precision=highest) > 0.5
    own_branch = (key_seg[None, :] == query_seg[:, None]) & (key_pos[None, :] <= query_pos[:, None])
    allowed = (key_pos < key_limit)[None, :] & (key_ancestor | own_branch)
    scores = (
        jnp.einsum("qhd,kd->hqk", queries, key_part, preferred_element_type=jnp.float32)
        * scale_factor
    )
    running_max = jnp.full((local_q, local_rows), -1e30, jnp.float32)
    piece_max = jnp.max(jnp.where(allowed[None], scores, -1e30), axis=-1)
    new_max = jnp.maximum(running_max, piece_max)
    numer = jnp.where(allowed[None], jnp.exp(scores - new_max[..., None]), 0.0)
    new_sum = jnp.sum(numer, axis=-1)
    new_acc = jnp.einsum(
        "hqk,kd->hqd", numer.astype(jnp.bfloat16), value_part, preferred_element_type=jnp.float32
    )
    folded = (new_max, new_sum, new_acc)
    running_max, running_sum, accum = folded
    result = accum / running_sum[..., None]
    result = jnp.swapaxes(result, 0, 1).reshape(local_rows, local_q * att_dim)
    att_out = jnp.where(valid[:, None], result, 0.0).astype(jnp.bfloat16)
    return (lin_mixed, att_out)


def solution(mesh):
    placed = (
        P(("rollout", "branch"), None),
        P("rollout"),
        P("rollout"),
        P(None, None, "tensor"),
        P(None, None, "tensor"),
        P("tensor"),
        P("tensor", None),
        P(),
        P(None, "tensor"),
        P(),
    )
    return jax.shard_map(
        on_device,
        mesh=mesh,
        in_specs=placed,
        out_specs=(P(("rollout", "branch", "tensor"), None), P(("rollout", "branch"), "tensor")),
        check_vma=False,
    )
```

profile of v0, /device:TPU:11, one launch (start us, length us, event | category | flops | bytes accessed | tf_op | source)
XLA Modules:
  0.0 533.6 jit_solution(16584756853319319458)
XLA Ops:
  8.6 3.4 fusion.50
  13.7 3.8 reduce_window_sum.13
  17.8 4.7 copy.173
  22.5 6.2 %fusion.48 = f32[1024,3,2,128]{3,0,2,1:T(8,128)S(1)} fusion(bf16[3,2,128,2048]{3,2,1,0:T(8,128)(2,1)} %bitcast.226, bf16[1024,2048]{1,0:T(8,128)(2,1)} %param.18), kind=kOutput, calls=%fused_computation.58 | convolution fusion | flops 3221225472 | bytes 10485760 | tf_op jit(solution)/shard_map/dot_general | solution.py:143
  28.7 1.9 multiply_reduce_fusion.1
  37.2 2.8 fusion.64
  40.0 158.7 %custom-call.4 = f32[4,4,2,1,64,64]{4,5,3,2,1,0:T(8,128)} custom-call(f32[4,4,2,1,64,64]{5,4,3,2,1,0:T(8,128)} %fusion.64), custom_call_target="InvertDiagBlocksLowerTriangular" | custom-call | tf_op jit(solution)/shard_map/vmap(jit(_solve_triangular))/vmap(vmap())/triangular_solve | solution.py:57
  198.6 3.5 fusion.52
  205.9 20.8 %while.44 = (s32[]{:T(128)}, f32[4,2,128,256]{3,2,1,0:T(8,128)S(1)}, f32[4,4,2]{1,2,0:T(2,128)S(1)}, f32[4,4,2,64,128]{4,3,2,1,0:T(8,128)}, f32[4,4,2,64,256]{4,...) while((s32[]{:T(128)}, f32[4,2,128,256]{3,2,1,0:T(8,128)S(1)}, f32[4,4,2]{1,2,0:T(2,128)S(1)}, ...), condition=%wide.region_4.5_spmd, body=%wide.region_3.4_spmd.sunk | while | flops 403308544 | bytes 5244157 | solution.py:109
  205.9 2.6 convolution_subtract_fusion.4
  208.7 2.4 convolution_add_fusion.9
  211.1 2.6 convolution_subtract_fusion.4
  213.9 2.4 convolution_add_fusion.9
  216.3 2.6 convolution_subtract_fusion.4
  219.1 2.4 convolution_add_fusion.9
  221.5 2.6 convolution_subtract_fusion.4
  224.3 2.4 convolution_add_fusion.9
  229.1 2.8 bitcast_multiply_fusion
  231.9 4.1 fusion.59
  236.0 13.5 %all-gather.6.cloned.1.call-done = f32[8,2,128,128]{3,2,1,0:T(8,128)} async-done(((f32[4,2,128,128]{3,2,1,0:T(8,128)}), f32[8,2,128,128]{3,2,1,0:T(8,128)}) %all-gather.6.cloned.1.call-update) | async-done | bytes 1048592 | tf_op jit(solution)/shard_map/all_gather | solution.py:178
  249.5 22.9 %all-gather.8.cloned.1.call-done = f32[8,2,128,128]{3,2,1,0:T(8,128)} async-done(((f32[4,2,128,128]{3,2,1,0:T(8,128)}), f32[8,2,128,128]{3,2,1,0:T(8,128)}) %all-gather.8.cloned.1.call-update) | async-done | bytes 1048592 | tf_op jit(solution)/shard_map/all_gather | solution.py:177
  272.5 31.7 %while.46 = (s32[]{:T(128)}, f32[8,2,128,128]{3,0,2,1:T(8,128)S(1)}, f32[8,2,128,128]{3,2,1,0:T(8,128)}, f32[8,2,128,128]{3,2,1,0:T(8,128)}, s32[8]{0:T(128)S(1)}, /*index=5*/pred[8]{0:T(512)(128)(4,1)S(1)}, s32[]{:T(128)}) while((s32[]{:T(128)}, f32[8,2,128,128]{3,0,2,1:T(8,128)S(1)}, f32[8,2,128,128]{3,2,1,0:T(8,128)}, ...), condition=%wide.region_6.7_spmd.clone, body=%wide.region_5.6_spmd.clone.sunk | while | flops 428081344 | bytes 6291573 | solution.py:185
  272.5 2.9 convolution_add_fusion.11
  275.4 1.6 convolution_bitcast_fusion.3
  277.0 2.9 convolution_add_fusion.11
  279.9 1.6 convolution_bitcast_fusion.3
  281.6 2.9 convolution_add_fusion.11
  284.5 1.6 convolution_bitcast_fusion.3
  286.1 2.9 convolution_add_fusion.11
  289.0 1.6 convolution_bitcast_fusion.3
  290.6 2.9 convolution_add_fusion.11
  293.5 1.6 convolution_bitcast_fusion.3
  295.2 2.9 convolution_add_fusion.11
  298.0 1.6 convolution_bitcast_fusion.3
  299.7 2.9 convolution_add_fusion.11
  302.6 1.6 convolution_bitcast_fusion.3
  304.4 29.4 %while.45 = (s32[]{:T(128)}, f32[4,2,128,128]{3,2,1,0:T(8,128)S(1)}, bf16[4,4,2,64,128]{4,3,2,1,0:T(8,128)(2,1)}, f32[4,4,2]{1,2,0:T(2,128)S(1)}, f32[4,4,2,64,1...) while((s32[]{:T(128)}, ...), condition=%wide.region_9.10_spmd, body=%wide.region_8.9_spmd.sunk | while | flops 352714752 | bytes 4983065 | solution.py:80
  305.9 1.6 convolution_subtract_fusion.5
  307.7 2.0 convolution_add_fusion.10
  309.7 2.0 fusion.183
  313.3 1.6 convolution_subtract_fusion.5
  315.0 2.0 convolution_add_fusion.10
  317.1 2.0 fusion.183
  320.6 1.6 convolution_subtract_fusion.5
  322.4 2.0 convolution_add_fusion.10
  324.4 2.0 fusion.183
  327.9 1.6 convolution_subtract_fusion.5
  329.7 2.0 convolution_add_fusion.10
  331.7 2.0 fusion.183
  335.3 5.8 %fusion.79 = f32[1024,2048]{1,0:T(8,128)} fusion(bf16[256,2048]{1,0:T(8,128)(2,1)} %param.24, bf16[128,8,2,128]{3,2,1,0:T(2,128)(2,1)S(1)} %bitcast.227, pred[1024]{0:T(1024)(128)(4,1)S(1)} %lt.81), kind=kOutput, calls=%fused_computation.107 | convolution fusion | flops 1074003968 | bytes 9962496 | tf_op jit(solution)/shard_map/dot_general | solution.py:191
  341.2 72.7 %reduce-scatter.2.cloned.1.call-done = f32[256,2048]{1,0:T(8,128)} async-done(((f32[1024,2048]{1,0:T(8,128)}), f32[256,2048]{1,0:T(8,128)}) %reduce-scatter.2.cloned.1.call-update) | async-done | bytes 2097168 | tf_op jit(solution)/shard_map/reduce_scatter | solution.py:197
  414.0 2.4 multiply_reduce_fusion
  416.5 2.9 multiply_convert_fusion
  419.7 3.5 copy.210
  427.4 6.4 %or_and_fusion = pred[1024,2048]{1,0:T(8,128)(4,1)} fusion(s32[2048]{0:T(1024)S(1)} %get-tuple-element.312, s32[2048]{0:T(1024)S(1)} %get-tuple-element.311, s32[1024]{0:T(1024)S(1)} %get-tuple-element.313, s32[1024]{0:T(1024)S(1)} %get-tuple-element.314, pred[2048]{0:T(1024)(128)(4,1)S(1)} %fusion.112, f32[1024,8]{1,0:T(8,128)S(1)} %bitcast.230), kind=kOutput, calls=%fused_computation.57 | convolution fusion | flops 213925888 | bytes 2156544 | tf_op jit(solution)/shard_map/dot_general | solution.py:226
  433.8 6.0 %copy.195 = pred[1024,2048]{0,1:T(8,128)(4,1)} copy(pred[1024,2048]{1,0:T(8,128)(4,1)} %or_and_fusion) | data formatting | bytes 4194304 | tf_op jit(solution)/shard_map/and | solution.py:228
  439.8 14.8 %all-gather.12.cloned.1.call-done = bf16[1024,2048]{1,0:T(8,128)(2,1)} async-done(((bf16[256,2048]{1,0:T(8,128)(2,1)}), bf16[1024,2048]{1,0:T(8,128)(2,1)}) %all-gather.12.cloned.1.call-update) | async-done | bytes 4194320 | tf_op jit(solution)/shard_map/all_gather | solution.py:206
  454.5 4.6 convolution_convert_fusion
  459.1 25.3 %all-gather.10.cloned.1.call-done = bf16[2048,512]{1,0:T(8,128)(2,1)} async-done(((bf16[256,512]{1,0:T(8,128)(2,1)}), bf16[2048,512]{1,0:T(8,128)(2,1)}) %all-gather.10.cloned.1.call-update) | async-done | bytes 2097168 | tf_op jit(solution)/shard_map/all_gather | solution.py:210
  484.4 5.2 fusion.40
  489.6 5.8 %copy-done.1 = f32[2048,1024,2]{1,0,2:T(8,128)} copy-done((f32[2048,1024,2]{1,0,2:T(8,128)}, f32[2048,1024,2]{1,0,2:T(8,128)S(1)}, u32[]{:S(2)}) %copy-start.1) | copy-done | bytes 16777240
  495.5 3.9 fusion.43
  499.4 14.8 %all-gather.14.cloned.1.call-done = bf16[2048,512]{1,0:T(8,128)(2,1)} async-done(((bf16[256,512]{1,0:T(8,128)(2,1)}), bf16[2048,512]{1,0:T(8,128)(2,1)}) %all-gather.14.cloned.1.call-update) | async-done | bytes 2097168 | tf_op jit(solution)/shard_map/all_gather | solution.py:216
  514.2 9.4 %bitcast_divide_fusion = bf16[1024,2,256]{0,2,1:T(8,128)(2,1)} fusion(f32[2048,1024,2]{1,0,2:T(8,128)} %copy-done.1, f32[2,1024]{1,0:T(2,128)S(1)} %broadcast_maximum_fusion, pred[1024,2048]{0,1:T(8,128)(4,1)} %copy.195, f32[1024,2]{0,1:T(2,128)S(1)} %bitcast.234, bf16[2048,512]{1,0:T(8,128)(2,1)} %all-gather.14.cloned.1.call-done, s32[]{:T(128)S(6)} %select_n.135), kind=kOutput, calls=%fused_computation.66 | convolution fusion | flops 2165309440 | bytes 20987908 | tf_op jit(solution)/shard_map/hqk,kd->hqd/dot_general | solution.py:238
  (147 shorter events, 33.6 us)
Async XLA Ops:
  7.2 447.4 %copy-start = (bf16[2048,512]{1,0:T(8,128)(2,1)S(1)}, bf16[2048,512]{1,0:T(8,128)(2,1)}, u32[]{:S(2)}) copy-start(bf16[2048,512]{1,0:T(8,128)(2,1)} %param.26) | copy-start | bytes 6291460
  7.2 5.5 %copy-start.12 = (s32[8]{0:T(128)S(1)}, s32[8]{0:T(128)}, u32[]{:S(2)}) copy-start(s32[8]{0:T(128)} %param.20) | copy-start | bytes 100
  7.2 6.4 %copy-start.16 = (f32[2]{0:T(128)S(1)}, f32[2]{0:T(128)}, u32[]{:S(2)}) copy-start(f32[2]{0:T(128)} %param.23) | copy-start | bytes 28
  7.2 242.3 %all-gather.6.cloned.1.call-start = ((), (), s32[]{:S(2)}) async-start(), calls=%async_computation.1 | async-start | bytes 1572864 | tf_op jit(solution)/shard_map/all_gather | solution.py:178
  12.7 9.8 %copy-start.17 = (s32[4]{0:T(128)}, s32[4]{0:T(128)S(1)}, u32[]{:S(2)}) copy-start(s32[4]{0:T(128)S(1)} %iota_add_fusion.1) | copy-start | bytes 52
  12.9 0.6 copy-start.14
  33.4 2.4 copy-start.7
  35.0 2.1 copy-start.8
  35.0 163.6 %copy-start.4 = (f32[4,4,2,64,128]{4,3,2,1,0:T(8,128)S(1)}, f32[4,4,2,64,128]{4,3,2,1,0:T(8,128)}, u32[]{:S(2)}) copy-start(f32[4,4,2,64,128]{4,3,2,1,0:T(8,128)} %get-tuple-element.284) | copy-start | bytes 3145732
  202.1 1.2 copy-start.11
  226.7 2.3 copy-start.15
  227.8 4.1 copy-start.5
  227.9 44.6 %all-gather.8.cloned.1.call-start = ((), (), s32[]{:S(2)}) async-start(), calls=%async_computation.2 | async-start | bytes 1572864 | tf_op jit(solution)/shard_map/all_gather | solution.py:177
  228.6 185.4 %reduce-scatter.2.cloned.1.call-start = ((), (), s32[]{:S(2)}) async-start(), calls=%async_computation.3 | async-start | bytes 10485760 | tf_op jit(solution)/shard_map/reduce_scatter | solution.py:197
  229.1 43.4 %copy-start.9 = (s32[8]{0:T(128)S(1)}, s32[8]{0:T(128)}, u32[]{:S(2)}) copy-start(s32[8]{0:T(128)} %param.19) | copy-start | bytes 100
  341.2 75.2 %copy-start.10 = (f32[2048]{0:T(1024)S(1)}, f32[2048]{0:T(1024)}, u32[]{:S(2)}) copy-start(f32[2048]{0:T(1024)} %param.25) | copy-start | bytes 24580
  341.2 113.4 %all-gather.12.cloned.1.call-start = ((), (), s32[]{:S(2)}) async-start(), calls=%async_computation.5 | async-start | bytes 5242880 | tf_op jit(solution)/shard_map/all_gather | solution.py:206
  414.0 2.5 copy-start.2
  419.4 64.9 %all-gather.10.cloned.1.call-start = ((), (), s32[]{:S(2)}) async-start(), calls=%async_computation.4 | async-start | bytes 2359296 | tf_op jit(solution)/shard_map/all_gather | solution.py:210
  419.7 3.5 copy-start.6
  423.2 2.3 copy-start.13
  423.2 3.9 copy-start.18
  425.4 88.8 %all-gather.14.cloned.1.call-start = ((), (), s32[]{:S(2)}) async-start(), calls=%async_computation.6 | async-start | bytes 2359296 | tf_op jit(solution)/shard_map/all_gather | solution.py:216
  484.4 11.1 %copy-start.3 = (pred[1024,2048]{0,1:T(8,128)(4,1)S(1)}, pred[1024,2048]{0,1:T(8,128)(4,1)}, u32[]{:S(2)}) copy-start(pred[1024,2048]{0,1:T(8,128)(4,1)} %copy.195) | copy-start | bytes 6291460
  489.6 5.8 %copy-start.1 = (f32[2048,1024,2]{1,0,2:T(8,128)}, f32[2048,1024,2]{1,0,2:T(8,128)S(1)}, u32[]{:S(2)}) copy-start(f32[2048,1024,2]{1,0,2:T(8,128)S(1)} %get-tuple-element.304) | copy-start | bytes 50331652
Sparse Core Ops, SparseCore 0:
  228.0 21.5 all-gather.5
  251.1 21.2 all-gather.7
  341.3 72.6 reduce-scatter.1
  419.6 34.9 all-gather.11
  456.4 27.8 all-gather.9
  486.3 27.8 all-gather.13
where the time goes:
time: 544 us; the launch traced here: 534 us
  other arithmetic  185 us (34%)
  waiting for transfers between devices  165 us (30%)
  matrix products  135 us (25%)
  local copies, waits for them, and re-layouts  32.6 us (6%)
  between operations  14.9 us (3%)
    another operation x2, other arithmetic, block_terms(): jax.scipy.linalg.solve_triangular(system, right_hand, lower=True, unit_di...  159 us
    reduce_scatter x1, waiting for transfers between devices, on_device(): lax.psum_scatter(partial_sum, 'tensor', scatter_dimension=0, tiled=True)  72.7 us
    all_gather x1, waiting for transfers between devices, on_device(): lax.all_gather(kv_rows[:, :half_cols], ('branch', 'tensor'), axis=0, tile...  25.3 us
    all_gather x1, waiting for transfers between devices, on_device(): lax.all_gather(own_offset, 'branch', axis=0, tiled=True)  22.9 us
    dot_general x7, matrix products, replay(): jnp.einsum('nhij,nhjv->nhiv', all_linear, starts, precision=highest)  20.1 us
    all_gather x1, waiting for transfers between devices, on_device(): lax.all_gather(kv_rows[:, half_cols:], ('branch', 'tensor'), axis=0, tile...  14.8 us
    unnamed x40, local copies, waits for them, and re-layouts  14.8 us
    all_gather x1, waiting for transfers between devices, on_device(): normed_full = lax.all_gather(normed_rows, 'tensor', axis=0, tiled=True)  14.8 us
  transfers between devices with their start and end apart: 6, of which 6 were waited for; matrix products, arithmetic and copies ran while one was open for 8% of the time, Pallas kernels for 0%

commit v1 on v0

v1 whole, which is shorter than its diff:
```python
import functools
import math

import jax
import jax.numpy as jnp
from jax import lax
from jax.experimental import pallas as pl
from jax.experimental.pallas import tpu as pltpu
from jax.sharding import PartitionSpec as P

KV_HEADS = 2
ATT_DIM = 256
SEG = 256
MIB = 1024 * 1024

f32 = jnp.float32
bf16 = jnp.bfloat16
highest = lax.Precision.HIGHEST
MESH = pl.DeviceIdType.MESH

NN = (((1,), (0,)), ((), ()))
NT = (((1,), (1,)), ((), ()))
TN = (((0,), (0,)), ((), ()))


def dot1(a, b, dims=NN):
    return lax.dot_general(a, b, dims, preferred_element_type=f32)


def split(x):
    high = x.astype(bf16)
    return high, (x - high.astype(f32)).astype(bf16)


def dot3(a, b, dims=NN):
    (ah, al), (bh, bl) = a, b
    return dot1(ah, bh, dims) + (dot1(ah, bl, dims) + dot1(al, bh, dims))


def unit_rows(matrix):
    return matrix * lax.rsqrt(jnp.sum(matrix * matrix, axis=-1, keepdims=True) + 1e-06)


def ancestor_table(parent_map):
    count = parent_map.shape[0]

    def widen(counter, table):
        return parent_map + jnp.dot(parent_map, table, precision=highest)

    return lax.fori_loop(0, count - 1, widen, parent_map)


def delta_kernel(heads, dim, lens_ref, rate_ref, tok_ref, w_ref, o1_ref, q2_ref, a_ref, b_ref):
    limit = lens_ref[pl.program_id(0)]
    proj = dot1(tok_ref[...], w_ref[...])
    rows = lax.broadcasted_iota(jnp.int32, (SEG, SEG), 0)
    cols = lax.broadcasted_iota(jnp.int32, (SEG, SEG), 1)
    strict = rows > cols
    inclusive = rows >= cols
    tril = inclusive.astype(f32)
    valid = lax.broadcasted_iota(jnp.int32, (SEG, 1), 0) < limit
    width = heads * dim
    eye = (rows == cols).astype(f32)
    parts = []
    for h in range(heads):
        q = unit_rows(proj[:, h * dim : (h + 1) * dim]) / math.sqrt(dim)
        k = unit_rows(proj[:, width + h * dim : width + (h + 1) * dim])
        v = proj[:, 2 * width + h * dim : 2 * width + (h + 1) * dim]
        g0 = proj[:, 3 * width + h : 3 * width + h + 1]
        g1 = proj[:, 3 * width + heads + h : 3 * width + heads + h + 1]
        beta = jnp.where(valid, 1.0 / (1.0 + jnp.exp(-g1)), 0.0)
        soft = jnp.maximum(g0, 0.0) + jnp.log1p(jnp.exp(-jnp.abs(g0)))
        step = jnp.where(valid, -rate_ref[h] * soft, 0.0)
        total = lax.dot_general(
            tril, jnp.broadcast_to(step, (SEG, dim)), NN, precision=highest,
            preferred_element_type=f32,
        )
        col = total[:, :1]
        row = total.T[:1, :]
        decay = jnp.exp(jnp.where(inclusive, col - row, 0.0))
        ks = split(k)
        key_key = dot3(ks, ks, NT)
        query_key = dot3(split(q), ks, NT)
        lower = jnp.where(strict, beta * decay * key_key, 0.0)
        mixing = jnp.where(inclusive, decay * query_key, 0.0)
        grown = jnp.exp(col)
        right = jnp.concatenate([beta * v, (beta * grown) * k], axis=1)
        last = total[SEG - 1 :, :]
        carried = jnp.exp(last - total) * k
        parts.append([lower, mixing, right, carried, grown * q, jnp.exp(last)])
    inverses = [eye - jnp.where(rows // 2 == cols // 2, p[0], 0.0) for p in parts]
    size = 2
    while size < SEG:
        pair = (rows // (2 * size) == cols // (2 * size)) & (rows // size != cols // size)
        halves = [split(x) for x in inverses]
        inner = [
            split(dot3(split(jnp.where(pair, p[0], 0.0)), x)) for p, x in zip(parts, halves)
        ]
        inverses = [x - dot3(xs, y) for x, xs, y in zip(inverses, halves, inner)]
        size *= 2
    small_eye = eye[:dim, :dim]
    for h in range(heads):
        lower, mixing, right, carried, queries, overall = parts[h]
        solved = split(dot3(split(inverses[h]), split(right)))
        out = dot3(split(mixing), solved)
        ends = dot3(split(carried), solved, TN)
        o1_ref[:, h * dim : (h + 1) * dim] = jnp.where(valid, out[:, :dim], 0.0)
        q2_ref[:, h * dim : (h + 1) * dim] = jnp.where(valid, queries - out[:, dim:], 0.0)
        b_ref[0, h] = ends[:, :dim]
        a_ref[0, h] = overall * small_eye - ends[:, dim:]


def delta_terms(tokens, weights, own_lengths, decay_rate, dim):
    heads = decay_rate.shape[0]
    rows, model = tokens.shape
    count = rows // SEG
    maps = jax.ShapeDtypeStruct((count, heads, dim, dim), f32)
    flat = jax.ShapeDtypeStruct((rows, heads * dim), f32)
    smem = pl.BlockSpec(memory_space=pltpu.SMEM)
    return pl.pallas_call(
        functools.partial(delta_kernel, heads, dim),
        grid=(count,),
        in_specs=[
            smem,
            smem,
            pl.BlockSpec((SEG, model), lambda s: (s, 0)),
            pl.BlockSpec(weights.shape, lambda s: (0, 0)),
        ],
        out_specs=[
            pl.BlockSpec((SEG, heads * dim), lambda s: (s, 0)),
            pl.BlockSpec((SEG, heads * dim), lambda s: (s, 0)),
            pl.BlockSpec((1, heads, dim, dim), lambda s: (s, 0, 0, 0)),
            pl.BlockSpec((1, heads, dim, dim), lambda s: (s, 0, 0, 0)),
        ],
        out_shape=[flat, flat, maps, maps],
        compiler_params=pltpu.CompilerParams(vmem_limit_bytes=40 * MIB),
    )(own_lengths, decay_rate, tokens, weights)


def mix_kernel(
    branches, tensors, parents_ref, a_ref, b_ref, o1_ref, q2_ref, lin_out_ref, tok_ref, gain_ref,
    mixed_ref, normed_ref,
    ends, ends16, starts, lin, total, end_send, end_recv, near_send, near_recv, far_send, far_recv,
    pass_send, pass_recv,
):
    me_b = lax.axis_index("branch")
    me_t = lax.axis_index("tensor")
    count, heads, dim, _ = a_ref.shape
    model = tok_ref.shape[1]
    chunk = mixed_ref.shape[0]
    chunks = lin.shape[1] // chunk
    width = heads * dim
    chips = tensors // 2
    chip, core = me_t // 2, me_t % 2
    partner = chip * 2 + (1 - core)
    ends[...] = jnp.zeros_like(ends)

    def far_of(f):
        return lax.rem(chip + 1 + f, chips)

    barrier = pltpu.get_barrier_semaphore()
    for d in range(1, branches):
        pl.semaphore_signal(
            barrier, inc=1, device_id={"branch": lax.rem(me_b + d, branches)}, device_id_type=MESH
        )
    pl.semaphore_signal(barrier, inc=1, device_id={"tensor": partner}, device_id_type=MESH)
    for f in range(chips - 1):
        pl.semaphore_signal(
            barrier, inc=1, device_id={"tensor": far_of(f) * 2 + core}, device_id_type=MESH
        )
    pl.semaphore_wait(barrier, branches - 1 + chips)

    first = me_b * count

    def end_copy(j, peer):
        return pltpu.make_async_remote_copy(
            src_ref=ends16.at[first + j], dst_ref=ends16.at[first + j],
            send_sem=end_send.at[j, peer], recv_sem=end_recv.at[first + j],
            device_id={"branch": peer}, device_id_type=MESH,
        )

    def take_end(s, carry):
        pltpu.make_async_remote_copy(
            src_ref=ends16.at[s], dst_ref=ends16.at[s],
            send_sem=end_send.at[0, 0], recv_sem=end_recv.at[s],
            device_id={"branch": lax.rem(me_b + 1, branches)}, device_id_type=MESH,
        ).wait_recv()
        ends[s] = ends16[s].astype(f32)
        return carry

    lax.fori_loop(0, first, take_end, 0)

    def advance(j, carry):
        s = first + j
        start = ends[parents_ref[s]]
        start = jnp.where(s > 0, start, jnp.zeros_like(start))
        starts[j] = start
        for h in range(heads):
            done = dot3(split(a_ref[j, h]), split(start[h])) + b_ref[j, h]
            ends[s, h] = done
            ends16[s, h] = done.astype(bf16)
        for peer in range(1, branches):
            @pl.when(me_b < peer)
            def _():
                end_copy(j, peer).start()
        return carry

    lax.fori_loop(0, count, advance, 0)

    def rows_of(i):
        return pl.ds(pl.multiple_of(i * chunk, chunk), chunk)

    def near_copy(i):
        return pltpu.make_async_remote_copy(
            src_ref=lin.at[me_t, rows_of(i)], dst_ref=lin.at[me_t, rows_of(i)],
            send_sem=near_send.at[i], recv_sem=near_recv.at[i],
            device_id={"tensor": partner}, device_id_type=MESH,
        )

    def far_copy(i, f):
        return pltpu.make_async_remote_copy(
            src_ref=lin.at[me_t, rows_of(i)], dst_ref=lin.at[me_t, rows_of(i)],
            send_sem=far_send.at[i, f], recv_sem=far_recv.at[i, f],
            device_id={"tensor": far_of(f) * 2 + core}, device_id_type=MESH,
        )

    def pass_copy(i, f):
        source = lax.rem(chip + chips - 1 - f, chips) * 2 + core
        return pltpu.make_async_remote_copy(
            src_ref=lin.at[source, rows_of(i)], dst_ref=lin.at[source, rows_of(i)],
            send_sem=pass_send.at[i, f], recv_sem=pass_recv.at[i, f],
            device_id={"tensor": partner}, device_id_type=MESH,
        )

    def produce(i, carry):
        j = (i * chunk) // SEG
        for h in range(heads):
            cols = slice(h * dim, (h + 1) * dim)
            out = o1_ref[rows_of(i), cols] + dot3(
                split(q2_ref[rows_of(i), cols]), split(starts[j, h])
            )
            lin[me_t, rows_of(i), cols] = out.astype(bf16)
        for f in range(chips - 1):
            far_copy(i, f).start()
        near_copy(i).start()
        return carry

    lax.fori_loop(0, chunks, produce, 0)

    def forward(i, carry):
        for f in range(chips - 1):
            far_copy(i, f).wait_recv()
            pass_copy(i, f).start()
        return carry

    tile = 512

    def mix(i, carry):
        forward(i, 0)
        near_copy(i).wait_recv()
        for f in range(chips - 1):
            pass_copy(i, f).wait_recv()

        def column(n, squares):
            cols = pl.ds(pl.multiple_of(n * tile, tile), tile)
            part = tok_ref[rows_of(i), cols].astype(f32)
            for t in range(tensors):
                part = part + dot1(
                    lin[t, rows_of(i), :], lin_out_ref[t * width : (t + 1) * width, cols]
                )
            total[:, cols] = part
            return squares + jnp.sum(part * part, axis=1, keepdims=True)

        squares = lax.fori_loop(0, model // tile, column, jnp.zeros((chunk, 1), f32))
        scale = lax.rsqrt(squares / model + 1e-06)
        normed_ref[rows_of(i), :] = (total[...] * scale * gain_ref[...]).astype(bf16)

        @pl.when(i == me_t)
        def _():
            mixed_ref[...] = total[...].astype(bf16)

        return carry

    lax.fori_loop(0, chunks, mix, 0)

    def finish(i, carry):
        near_copy(i).wait_send()
        for f in range(chips - 1):
            far_copy(i, f).wait_send()
            pass_copy(i, f).wait_send()
        return carry

    lax.fori_loop(0, chunks, finish, 0)

    def finish_ends(j, carry):
        for peer in range(1, branches):
            @pl.when(me_b < peer)
            def _():
                end_copy(j, peer).wait_send()
        return carry

    lax.fori_loop(0, count, finish_ends, 0)


def mix_rows(parents, amap, bmap, o1, q2, lin_out, tokens, gain):
    branches, tensors = lax.axis_size("branch"), lax.axis_size("tensor")
    count, heads, dim, _ = amap.shape
    rows, model = tokens.shape
    chunk = rows // tensors
    chunks = tensors
    segments = branches * count
    fars = max(tensors // 2 - 1, 1)
    vmem = pl.BlockSpec(memory_space=pltpu.VMEM)
    dma = pltpu.SemaphoreType.DMA
    return pl.pallas_call(
        functools.partial(mix_kernel, branches, tensors),
        in_specs=[pl.BlockSpec(memory_space=pltpu.SMEM)] + [vmem] * 7,
        out_specs=[vmem, vmem],
        out_shape=[
            jax.ShapeDtypeStruct((chunk, model), bf16),
            jax.ShapeDtypeStruct((rows, model), bf16),
        ],
        scratch_shapes=[
            pltpu.VMEM((segments, heads, dim, dim), f32),
            pltpu.VMEM((segments, heads, dim, dim), bf16),
            pltpu.VMEM((count, heads, dim, dim), f32),
            pltpu.VMEM((tensors, rows, heads * dim), bf16),
            pltpu.VMEM((chunk, model), f32),
            dma((count, branches)),
            dma((segments,)),
            dma((chunks,)),
            dma((chunks,)),
            dma((chunks, fars)),
            dma((chunks, fars)),
            dma((chunks, fars)),
            dma((chunks, fars)),
        ],
        compiler_params=pltpu.CompilerParams(
            collective_id=0, has_side_effects=True, vmem_limit_bytes=56 * MIB
        ),
    )(parents, amap, bmap, o1, q2, lin_out, tokens, gain)


def on_device(
    tokens, parents, lengths, lin_qkv, lin_gates, decay_rate, lin_out, norm_gain, att_q, att_kv
):
    branch_idx = lax.axis_index("branch")
    tensor_count = lax.axis_size("tensor")
    tensor_idx = lax.axis_index("tensor")
    local_rows, model_width = tokens.shape
    local_count = local_rows // SEG
    segment_count = lax.axis_size("branch") * local_count
    local_heads = decay_rate.shape[0]
    head_dim = lin_qkv.shape[2] // local_heads
    att_dim = ATT_DIM
    first_seg = branch_idx * local_count
    full_out = lax.all_gather(lin_out, "tensor", axis=0, tiled=True)
    own_lengths = lax.dynamic_slice_in_dim(lengths, first_seg, local_count, 0)
    weights = jnp.concatenate(
        [
            lin_qkv.reshape(model_width, -1),
            lin_gates.reshape(model_width, -1),
            jnp.zeros((model_width, 128 - 2 * local_heads), bf16),
        ],
        axis=1,
    )
    o1, q2, amap, bmap = delta_terms(tokens, weights, own_lengths, decay_rate, head_dim)
    lin_mixed, normed = mix_rows(
        parents, amap, bmap, o1, q2, full_out, tokens, norm_gain[None, :]
    )
    return attend(lin_mixed, normed, parents, lengths, att_q, att_kv)


def attend(lin_mixed, normed, parents, lengths, att_q, att_kv):
    branch_idx = lax.axis_index("branch")
    tensor_count = lax.axis_size("tensor")
    tensor_idx = lax.axis_index("tensor")
    local_rows, model_width = normed.shape
    local_count = local_rows // SEG
    segment_count = lax.axis_size("branch") * local_count
    first_seg = branch_idx * local_count
    att_dim = ATT_DIM
    seg_ids = jnp.arange(segment_count)
    local_flag = seg_ids[None, :] == (first_seg + jnp.arange(local_count))[:, None]
    own_lengths = jnp.sum(jnp.where(local_flag, lengths[None, :], 0), axis=1)
    valid = (jnp.arange(SEG)[None, :] < own_lengths[:, None]).reshape(local_rows)
    row_local = jnp.arange(local_rows)
    query_seg = first_seg + row_local // SEG
    query_pos = row_local % SEG
    parent_map = ((parents[:, None] == seg_ids[None, :]) & (seg_ids[:, None] > 0)).astype(f32)
    ancestry = ancestor_table(parent_map)
    local_anc = (jnp.dot(local_flag.astype(f32), ancestry, precision=highest) > 0.5).astype(f32)
    query_anc = jnp.repeat(local_anc, SEG, axis=0)
    local_q = att_q.shape[1] // att_dim
    kv_head = tensor_idx // (tensor_count // KV_HEADS)
    scale_factor = 1.0 / math.sqrt(att_dim)
    own_kv = lax.dynamic_slice_in_dim(att_kv, kv_head * att_dim, att_dim, 2)
    kv = jnp.dot(normed, own_kv.reshape(model_width, -1), preferred_element_type=f32).astype(bf16)
    full_kv = lax.all_gather(kv, "branch", axis=0, tiled=True)
    key_part, value_part = full_kv[:, :att_dim], full_kv[:, att_dim:]
    queries = jnp.dot(normed, att_q, preferred_element_type=f32).astype(bf16)
    queries = queries.reshape(local_rows, local_q, att_dim)
    global_rows = jnp.arange(key_part.shape[0])
    key_seg = global_rows // SEG
    key_pos = global_rows % SEG
    match = key_seg[:, None] == seg_ids[None, :]
    key_limit = jnp.sum(jnp.where(match, lengths[None, :], 0), axis=1)
    key_ancestor = jnp.dot(query_anc, match.astype(f32).T, precision=highest) > 0.5
    own_branch = (key_seg[None, :] == query_seg[:, None]) & (key_pos[None, :] <= query_pos[:, None])
    allowed = (key_pos < key_limit)[None, :] & (key_ancestor | own_branch)
    scores = (
        jnp.einsum("qhd,kd->hqk", queries, key_part, preferred_element_type=f32) * scale_factor
    )
    top = jnp.max(jnp.where(allowed[None], scores, -1e30), axis=-1)
    numer = jnp.where(allowed[None], jnp.exp(scores - top[..., None]), 0.0)
    sums = jnp.sum(numer, axis=-1)
    accum = jnp.einsum("hqk,kd->hqd", numer.astype(bf16), value_part, preferred_element_type=f32)
    result = accum / sums[..., None]
    result = jnp.swapaxes(result, 0, 1).reshape(local_rows, local_q * att_dim)
    att_out = jnp.where(valid[:, None], result, 0.0).astype(bf16)
    return (lin_mixed, att_out)


def solution(mesh):
    placed = (
        P(("rollout", "branch"), None),
        P("rollout"),
        P("rollout"),
        P(None, None, "tensor"),
        P(None, None, "tensor"),
        P("tensor"),
        P("tensor", None),
        P(),
        P(None, "tensor"),
        P(),
    )
    return jax.shard_map(
        on_device,
        mesh=mesh,
        in_specs=placed,
        out_specs=(P(("rollout", "branch", "tensor"), None), P(("rollout", "branch"), "tensor")),
        check_vma=False,
    )
```

time: 544 us -> 174 us (0.32); the launches traced: 534 us -> 171 us
  other arithmetic: 185 us -> 4.57 us
  waiting for transfers between devices: 165 us -> 15.8 us
  matrix products: 135 us -> 37.4 us
  Pallas kernels: 0 us -> 69.4 us
    another operation x5 -> x0, other arithmetic: 163 us -> none  [the longest x2 159 us: block_terms(): jax.scipy.linalg.solve_triangular(system, right_hand, lower=True, unit_di...]
    dot_general x49 -> x5, matrix products: 130 us -> 23.5 us  [the longest x1 6.95 us: attend(): jnp.einsum('hqk,kd->hqd', numer.astype(bf16), value_part, preferred_eleme...]
    all_gather x5 -> x2, waiting for transfers between devices: 91.3 us -> 15.1 us  [the longest x1 15.1 us: attend(): full_kv = lax.all_gather(kv, 'branch', axis=0, tiled=True)]
    reduce_scatter x1 -> x0, waiting for transfers between devices: 72.7 us -> none  [on_device(): lax.psum_scatter(partial_sum, 'tensor', scatter_dimension=0, tiled=True)]
    pallas_call x0 -> x2, Pallas kernels: none -> 69.4 us  [the longest x1 36.1 us: mix_rows(): pl.pallas_call(functools.partial(mix_kernel, branches, tensors), in_specs...]
    sub x0 -> x1, matrix products: none -> 12.5 us  [attend(): numer = jnp.where(allowed[None], jnp.exp(scores - top[..., None]), 0.0)]
    reduce_sum x5 -> x2, other arithmetic: 8.49 us -> 0.27 us  [the longest x1 0.18 us: attend(): own_lengths = jnp.sum(jnp.where(local_flag, lengths[None, :], 0), axis=1)]
    mul x5 -> x0, other arithmetic: 6.33 us -> none  [the longest x1 2.83 us: block_terms(): scaled_queries = jnp.exp(decay_blk)[..., None] * queries]
  transfers between devices with their start and end apart: 6 -> 2, of which waited for: 6 -> 1; matrix products, arithmetic and copies ran while one was open for 8% -> 22% of each run, Pallas kernels for 0% -> 19%
where the time goes in v1:
time: 174 us; the launch traced here: 171 us
  Pallas kernels  69.4 us (40%)
  matrix products  37.4 us (21%)
  local copies, waits for them, and re-layouts  29.6 us (17%)
  waiting for transfers between devices  15.8 us (9%)
  between operations  14.2 us (8%)
  other arithmetic  4.57 us (3%)
    pallas_call x1, Pallas kernels, mix_rows(): pl.pallas_call(functools.partial(mix_kernel, branches, tensors), in_specs...  36.1 us
    pallas_call x1, Pallas kernels, delta_terms(): pl.pallas_call(functools.partial(delta_kernel, heads, dim), grid=(count,)...  33.3 us
    all_gather x1, waiting for transfers between devices, attend(): full_kv = lax.all_gather(kv, 'branch', axis=0, tiled=True)  15.1 us
    unnamed x23, local copies, waits for them, and re-layouts  12.7 us
    sub x1, matrix products, attend(): numer = jnp.where(allowed[None], jnp.exp(scores - top[..., None]), 0.0)  12.5 us
    dot_general x1, matrix products, attend(): jnp.einsum('hqk,kd->hqd', numer.astype(bf16), value_part, preferred_eleme...  6.95 us
    dot_general x1, matrix products, attend(): jnp.dot(query_anc, match.astype(f32).T, precision=highest) > 0.5  6.31 us
    and x1, local copies, waits for them, and re-layouts, attend(): allowed = (key_pos < key_limit)[None, :] & (key_ancestor | own_branch)  6.07 us
  transfers between devices with their start and end apart: 2, of which 1 were waited for; matrix products, arithmetic and copies ran while one was open for 22% of the time, Pallas kernels for 19%

profile of v1, /device:TPU:11, one launch (start us, length us, event | category | flops | bytes accessed | tf_op | source)
XLA Modules:
  0.0 171.1 jit_solution(4358417638931146910)
XLA Ops:
  7.2 0.0 copy-start
  7.2 0.0 all-gather.3.cloned.1.call-start
  7.2 0.7 all-gather.3.cloned.1.call-update
  7.9 0.0 all-gather.5.cloned.1.call-start
  8.0 0.7 reshape.115
  8.7 0.4 copy.29
  9.1 4.8 %copy.27 = bf16[2048,3,256]{0,2,1:T(8,128)(2,1)} copy(bf16[2048,3,256]{2,0,1:T(8,128)(2,1)} %param.15) | data formatting | bytes 6291456 | tf_op args[3]
  13.8 4.7 %copy.28 = bf16[2048,768]{1,0:T(8,128)(2,1)} copy(bf16[2048,768]{0,1:T(8,128)(2,1)} %bitcast.53) | data formatting | bytes 6291456 | tf_op jit(solution)/shard_map/reshape | solution.py:361
  18.5 0.0 copy-start.9
  18.5 3.4 %constant_dynamic-slice_fusion = bf16[2048,2,256]{2,1,0:T(2,128)(2,1)S(1)} fusion(bf16[2048,2,512]{2,1,0:T(2,128)(2,1)} %param.21, s32[]{:T(128)S(6)} %select_n.89), kind=kLoop, calls=%fused_computation.66 | loop fusion | bytes 4194308 | tf_op jit(solution)/shard_map/dynamic_slice | solution.py:397
  21.9 1.9 %copy.39 = bf16[256,8,2,256]{3,1,2,0:T(8,128)(2,1)} copy(bf16[256,8,2,256]{3,2,1,0:T(2,128)(2,1)S(1)} %bitcast.54) | data formatting | bytes 4194304
  23.8 0.0 copy-start.6
  23.8 0.0 copy-done.9
  23.8 0.0 copy-start.1
  23.8 0.1 dynamic_slice.6.lens_ref
  23.9 0.1 pad.2.clone
  23.9 2.8 %maximum_maximum_fusion.w_ref = bf16[2048,896]{1,0:T(8,128)(2,1)S(1)} fusion(bf16[2048,4]{1,0:T(8,128)(2,1)S(1)} %copy.29, bf16[2048,768]{1,0:T(8,128)(2,1)} %copy.28, bf16[896]{0:T(1024)(128)(2,1)S(1)} %pad.2.clone), kind=kLoop, calls=%fused_computation.20 | loop fusion | flops 11010048 | bytes 6833920 | tf_op jit(solution)/shard_map/concatenate | solution.py:359
  26.8 0.0 copy-done.6
  26.8 0.2 copy-done.1
  27.0 0.0 copy-start.8
  27.0 33.3 %shard_map.113 = (f32[1024,256]{1,0:T(8,128)S(1)}, f32[1024,256]{1,0:T(8,128)S(1)}, f32[4,2,128,128]{3,2,1,0:T(8,128)S(1)}, f32[4,2,128,128]{3,2,1,0:T(8,128)S(1)}) custom-call(s32[4]{0:T(128)S(1)} %dynamic_slice.6.lens_ref, f32[2]{0:T(128)S(1)} %copy-done.6, bf16[1024,2048]{1,0:T(8,128)(2,1)S(1)} %copy-done.1, bf16[2048,896]{1,0:T(8,128)(2,1)S(1)} %maximum_maximum_fusion.w_ref), custom_call_target="tpu_custom_call" | custom-call | tf_op jit(solution)/shard_map/pallas_call | solution.py:120
  60.3 0.0 copy-start.2
  60.3 1.0 copy-done.2
  61.3 0.0 copy-start.3
  61.3 1.0 copy-done.3
  62.2 0.0 copy-start.4
  62.2 0.8 copy-done.4
  63.0 0.0 copy-start.5
  63.0 0.8 copy-done.5
  63.9 0.0 copy-done.8
  63.9 0.1 fusion.38
  63.9 1.5 while.11
  63.9 0.2 convolution_add_fusion.2
  64.2 0.2 convolution_add_fusion.2
  64.4 0.2 convolution_add_fusion.2
  64.6 0.2 convolution_add_fusion.2
  64.8 0.2 convolution_add_fusion.2
  65.0 0.2 convolution_add_fusion.2
  65.2 0.2 convolution_add_fusion.2
  65.4 0.2 fusion.21
  65.6 0.0 all-gather.3.cloned.1.call-done.lin_out_ref
  65.6 0.0 copy-start.7
  65.6 36.1 %shard_map.114 = (bf16[256,2048]{1,0:T(8,128)(2,1)}, bf16[1024,2048]{1,0:T(8,128)(2,1)}) custom-call(s32[8]{0:T(128)S(1)} %get-tuple-element.111, f32[4,2,128,128]{3,2,1,0:T(8,128)} %copy-done.4, f32[4,2,128,128]{3,2,1,0:T(8,128)} %copy-done.5, f32[1024,256]{1,0:T(8,128)} %copy-done.2, f32[1024,256]{1,0:T(8,128)} %copy-done.3, ...), custom_call_target="tpu_custom_call" | custom-call | tf_op jit(solution)/shard_map/pallas_call | solution.py:315
  101.8 0.0 copy-done.7
  101.8 5.5 %convolution_convert_fusion.1 = bf16[1024,512]{1,0:T(8,128)(2,1)} fusion(bf16[1024,2048]{1,0:T(8,128)(2,1)} %get-tuple-element.31, bf16[2048,512]{1,0:T(8,128)(2,1)S(1)} %bitcast.55), kind=kOutput, calls=%fused_computation.25 | convolution fusion | flops 2148007936 | bytes 7340032 | tf_op jit(solution)/shard_map/dot_general | solution.py:398
  107.3 0.0 all-gather.5.cloned.1.call-update
  107.3 0.1 select_reduce_fusion
  107.4 6.3 %or_and_fusion = pred[1024,2048]{1,0:T(8,128)(4,1)} fusion(s32[2048]{0:T(1024)S(1)} %get-tuple-element.55, s32[2048]{0:T(1024)S(1)} %get-tuple-element.54, s32[1024]{0:T(1024)S(1)} %get-tuple-element.56, s32[1024]{0:T(1024)S(1)} %get-tuple-element.57, pred[2048]{0:T(1024)(128)(4,1)S(1)} %fusion.39, f32[1024,8]{1,0:T(8,128)S(1)} %bitcast.57), kind=kOutput, calls=%fused_computation.19 | convolution fusion | flops 213925888 | bytes 2156544 | tf_op jit(solution)/shard_map/dot_general | solution.py:408
  113.7 6.1 %copy.30 = pred[1024,2048]{0,1:T(8,128)(4,1)} copy(pred[1024,2048]{1,0:T(8,128)(4,1)} %or_and_fusion) | data formatting | bytes 4194304 | tf_op jit(solution)/shard_map/and | solution.py:410
  119.8 0.2 select_reduce_fusion.1
  120.0 0.1 iota_compare_fusion.4
  120.1 0.0 copy-done
  120.1 4.6 %convolution_convert_fusion = bf16[1024,512]{0,1:T(8,128)(2,1)S(1)} fusion(bf16[1024,2048]{1,0:T(8,128)(2,1)} %get-tuple-element.31, bf16[2048,512]{1,0:T(8,128)(2,1)S(1)} %copy-done), kind=kOutput, calls=%fused_computation.24 | convolution fusion | flops 2148007936 | bytes 7340032 | tf_op jit(solution)/shard_map/dot_general | solution.py:401
  124.7 15.1 %all-gather.5.cloned.1.call-done = bf16[2048,512]{1,0:T(8,128)(2,1)} async-done(((bf16[1024,512]{1,0:T(8,128)(2,1)}), bf16[2048,512]{1,0:T(8,128)(2,1)}) %all-gather.5.cloned.1.call-update) | async-done | bytes 2097168 | tf_op jit(solution)/shard_map/all_gather | solution.py:399
  139.7 12.5 %fusion.43 = (f32[2,1024]{1,0:T(2,128)S(1)}, bf16[2,1024,2048]{1,2,0:T(8,128)(2,1)}) fusion(pred[1024,2048]{0,1:T(8,128)(4,1)} %copy.30, bf16[1024,2,256]{0,2,1:T(8,128)(2,1)S(1)} %bitcast.59, bf16[2048,512]{1,0:T(8,128)(2,1)} %all-gather.5.cloned.1.call-done), kind=kOutput, calls=%fused_computation.69 | convolution fusion | flops 4324329472 | bytes 16785408 | tf_op jit(solution)/shard_map/sub | solution.py:415
  152.2 7.0 %bitcast_divide_fusion = bf16[1024,2,256]{0,2,1:T(8,128)(2,1)} fusion(bf16[2,1024,2048]{1,2,0:T(8,128)(2,1)} %get-tuple-element.53, bf16[2048,512]{1,0:T(8,128)(2,1)} %all-gather.5.cloned.1.call-done, f32[1024,2]{0,1:T(2,128)S(1)} %bitcast.60), kind=kOutput, calls=%fused_computation.21 | convolution fusion | flops 2148532224 | bytes 10493952 | tf_op jit(solution)/shard_map/hqk,kd->hqd/dot_general | solution.py:417
  159.2 1.5 copy.34
  160.7 1.3 select_convert_fusion
  162.0 2.3 %copy.50 = bf16[256,2048]{1,0:T(8,128)(2,1)} copy(bf16[256,2048]{1,0:T(8,128)(2,1)} %get-tuple-element.102) | data formatting | bytes 2097152
  (15 shorter events, 0.1 us)
Async XLA Ops:
  7.2 112.9 %copy-start = (bf16[2048,512]{1,0:T(8,128)(2,1)S(1)}, bf16[2048,512]{1,0:T(8,128)(2,1)}, u32[]{:S(2)}) copy-start(bf16[2048,512]{1,0:T(8,128)(2,1)} %param.20) | copy-start | bytes 6291460
  7.2 58.4 %all-gather.3.cloned.1.call-start = ((), (), s32[]{:S(2)}) async-start(), calls=%async_computation | async-start | bytes 5242880 | tf_op jit(solution)/shard_map/all_gather | solution.py:357
  7.9 131.8 %all-gather.5.cloned.1.call-start = ((), (), s32[]{:S(2)}) async-start(), calls=%async_computation.1 | async-start | bytes 3145728 | tf_op jit(solution)/shard_map/all_gather | solution.py:399
  18.5 5.3 %copy-start.9 = (s32[8]{0:T(128)S(1)}, s32[8]{0:T(128)}, u32[]{:S(2)}) copy-start(s32[8]{0:T(128)} %param.14) | copy-start | bytes 100
  23.8 3.0 %copy-start.6 = (f32[2]{0:T(128)S(1)}, f32[2]{0:T(128)}, u32[]{:S(2)}) copy-start(f32[2]{0:T(128)} %rate_ref.1) | copy-start | bytes 28
  23.8 3.2 %copy-start.1 = (bf16[1024,2048]{1,0:T(8,128)(2,1)S(1)}, bf16[1024,2048]{1,0:T(8,128)(2,1)}, u32[]{:S(2)}) copy-start(bf16[1024,2048]{1,0:T(8,128)(2,1)} %tok_ref.3) | copy-start | bytes 12582916
  27.0 36.9 %copy-start.8 = (s32[8]{0:T(128)S(1)}, s32[8]{0:T(128)}, u32[]{:S(2)}) copy-start(s32[8]{0:T(128)} %parents_ref.1) | copy-start | bytes 100
  60.3 1.0 copy-start.2
  61.3 1.0 copy-start.3
  62.2 0.8 copy-start.4
  63.0 0.8 copy-start.5
  65.6 36.1 %copy-start.7 = (bf16[256,8,2,256]{3,1,2,0:T(8,128)(2,1)S(1)}, bf16[256,8,2,256]{3,1,2,0:T(8,128)(2,1)}, u32[]{:S(2)}) copy-start(bf16[256,8,2,256]{3,1,2,0:T(8,128)(2,1)} %copy.39) | copy-start | bytes 6291460
Sparse Core Ops, SparseCore 0:
  9.6 36.0 all-gather.2
  107.4 32.2 all-gather.4

commit v2 on v1

--- a/solution.py
+++ b/solution.py
@@ -34,7 +34,10 @@
 
 def dot3(a, b, dims=NN):
     (ah, al), (bh, bl) = a, b
-    return dot1(ah, bh, dims) + (dot1(ah, bl, dims) + dot1(al, bh, dims))
+    ax, bx = dims[0][0][0], dims[0][1][0]
+    left = jnp.concatenate([ah, ah, al], axis=ax)
+    right = jnp.concatenate([bh, bl, bh], axis=bx)
+    return dot1(left, right, dims)
 
 
 def unit_rows(matrix):
@@ -50,90 +53,107 @@
     return lax.fori_loop(0, count - 1, widen, parent_map)
 
 
-def delta_kernel(heads, dim, lens_ref, rate_ref, tok_ref, w_ref, o1_ref, q2_ref, a_ref, b_ref):
-    limit = lens_ref[pl.program_id(0)]
-    proj = dot1(tok_ref[...], w_ref[...])
+def delta_kernel(
+    heads, dim, per, lens_ref, rate_ref, tok_ref, w_ref, o1_ref, q2_ref, a_ref, b_ref
+):
+    proj_all = dot1(tok_ref[...], w_ref[...])
+    half = SEG // 2
     rows = lax.broadcasted_iota(jnp.int32, (SEG, SEG), 0)
     cols = lax.broadcasted_iota(jnp.int32, (SEG, SEG), 1)
     strict = rows > cols
     inclusive = rows >= cols
     tril = inclusive.astype(f32)
-    valid = lax.broadcasted_iota(jnp.int32, (SEG, 1), 0) < limit
+    hrows = lax.broadcasted_iota(jnp.int32, (half, half), 0)
+    hcols = lax.broadcasted_iota(jnp.int32, (half, half), 1)
+    places = lax.broadcasted_iota(jnp.int32, (SEG, 1), 0)
     width = heads * dim
-    eye = (rows == cols).astype(f32)
+    eye = (hrows == hcols).astype(f32)
     parts = []
-    for h in range(heads):
-        q = unit_rows(proj[:, h * dim : (h + 1) * dim]) / math.sqrt(dim)
-        k = unit_rows(proj[:, width + h * dim : width + (h + 1) * dim])
-        v = proj[:, 2 * width + h * dim : 2 * width + (h + 1) * dim]
-        g0 = proj[:, 3 * width + h : 3 * width + h + 1]
-        g1 = proj[:, 3 * width + heads + h : 3 * width + heads + h + 1]
-        beta = jnp.where(valid, 1.0 / (1.0 + jnp.exp(-g1)), 0.0)
-        soft = jnp.maximum(g0, 0.0) + jnp.log1p(jnp.exp(-jnp.abs(g0)))
-        step = jnp.where(valid, -rate_ref[h] * soft, 0.0)
-        total = lax.dot_general(
-            tril, jnp.broadcast_to(step, (SEG, dim)), NN, precision=highest,
-            preferred_element_type=f32,
-        )
-        col = total[:, :1]
-        row = total.T[:1, :]
-        decay = jnp.exp(jnp.where(inclusive, col - row, 0.0))
-        ks = split(k)
-        key_key = dot3(ks, ks, NT)
-        query_key = dot3(split(q), ks, NT)
-        lower = jnp.where(strict, beta * decay * key_key, 0.0)
-        mixing = jnp.where(inclusive, decay * query_key, 0.0)
-        grown = jnp.exp(col)
-        right = jnp.concatenate([beta * v, (beta * grown) * k], axis=1)
-        last = total[SEG - 1 :, :]
-        carried = jnp.exp(last - total) * k
-        parts.append([lower, mixing, right, carried, grown * q, jnp.exp(last)])
-    inverses = [eye - jnp.where(rows // 2 == cols // 2, p[0], 0.0) for p in parts]
+    for g in range(per):
+        valid = places < lens_ref[pl.program_id(0) * per + g]
+        proj = proj_all[g * SEG : (g + 1) * SEG]
+        for h in range(heads):
+            q = unit_rows(proj[:, h * dim : (h + 1) * dim]) / math.sqrt(dim)
+            k = unit_rows(proj[:, width + h * dim : width + (h + 1) * dim])
+            v = proj[:, 2 * width + h * dim : 2 * width + (h + 1) * dim]
+            g0 = proj[:, 3 * width + h : 3 * width + h + 1]
+            g1 = proj[:, 3 * width + heads + h : 3 * width + heads + h + 1]
+            beta = jnp.where(valid, 1.0 / (1.0 + jnp.exp(-g1)), 0.0)
+            soft = jnp.maximum(g0, 0.0) + jnp.log1p(jnp.exp(-jnp.abs(g0)))
+            step = jnp.where(valid, -rate_ref[h] * soft, 0.0)
+            total = lax.dot_general(
+                tril, jnp.broadcast_to(step, (SEG, dim)), NN, precision=highest,
+                preferred_element_type=f32,
+            )
+            col = total[:, :1]
+            row = total.T[:1, :]
+            decay = jnp.exp(jnp.where(inclusive, col - row, 0.0))
+            ks = split(k)
+            key_key = dot3(ks, ks, NT)
+            query_key = dot3(split(q), ks, NT)
+            lower = jnp.where(strict, beta * decay * key_key, 0.0)
+            mixing = jnp.where(inclusive, decay * query_key, 0.0)
+            grown = jnp.exp(col)
+            right = jnp.concatenate([beta * v, (beta * grown) * k], axis=1)
+            last = total[SEG - 1 :, :]
+            carried = jnp.exp(last - total) * k
+            parts.append([lower, mixing, right, carried, grown * q, jnp.exp(last), valid])
+    lowers = [
+        p[0][c * half : (c + 1) * half, c * half : (c + 1) * half] for p in parts for c in range(2)
+    ]
+    inverses = [eye - jnp.where(hrows // 2 == hcols // 2, x, 0.0) for x in lowers]
     size = 2
-    while size < SEG:
-        pair = (rows // (2 * size) == cols // (2 * size)) & (rows // size != cols // size)
+    while size < half:
+        pair = (hrows // (2 * size) == hcols // (2 * size)) & (hrows // size != hcols // size)
         halves = [split(x) for x in inverses]
         inner = [
-            split(dot3(split(jnp.where(pair, p[0], 0.0)), x)) for p, x in zip(parts, halves)
+            split(dot3(split(jnp.where(pair, x, 0.0)), y)) for x, y in zip(lowers, halves)
         ]
         inverses = [x - dot3(xs, y) for x, xs, y in zip(inverses, halves, inner)]
         size *= 2
-    small_eye = eye[:dim, :dim]
-    for h in range(heads):
-        lower, mixing, right, carried, queries, overall = parts[h]
-        solved = split(dot3(split(inverses[h]), split(right)))
-        out = dot3(split(mixing), solved)
-        ends = dot3(split(carried), solved, TN)
-        o1_ref[:, h * dim : (h + 1) * dim] = jnp.where(valid, out[:, :dim], 0.0)
-        q2_ref[:, h * dim : (h + 1) * dim] = jnp.where(valid, queries - out[:, dim:], 0.0)
-        b_ref[0, h] = ends[:, :dim]
-        a_ref[0, h] = overall * small_eye - ends[:, dim:]
+    inverses = [split(x) for x in inverses]
+    for g in range(per):
+        for h in range(heads):
+            n = g * heads + h
+            lower, mixing, right, carried, queries, overall, valid = parts[n]
+            upper = dot3(inverses[2 * n], split(right[:half]))
+            rest = right[half:] - dot3(split(lower[half:, :half]), split(upper))
+            bottom = dot3(inverses[2 * n + 1], split(rest))
+            solved = split(jnp.concatenate([upper, bottom], axis=0))
+            out = dot3(split(mixing), solved)
+            ends = dot3(split(carried), solved, TN)
+            at = slice(g * SEG, (g + 1) * SEG)
+            o1_ref[at, h * dim : (h + 1) * dim] = jnp.where(valid, out[:, :dim], 0.0)
+            q2_ref[at, h * dim : (h + 1) * dim] = jnp.where(valid, queries - out[:, dim:], 0.0)
+            b_ref[g, h] = ends[:, :dim]
+            a_ref[g, h] = overall * eye - ends[:, dim:]
 
 
 def delta_terms(tokens, weights, own_lengths, decay_rate, dim):
     heads = decay_rate.shape[0]
     rows, model = tokens.shape
     count = rows // SEG
+    per = 2 - count % 2
     maps = jax.ShapeDtypeStruct((count, heads, dim, dim), f32)
     flat = jax.ShapeDtypeStruct((rows, heads * dim), f32)
     smem = pl.BlockSpec(memory_space=pltpu.SMEM)
     return pl.pallas_call(
-        functools.partial(delta_kernel, heads, dim),
-        grid=(count,),
+        functools.partial(delta_kernel, heads, dim, per),
+        grid=(count // per,),
         in_specs=[
             smem,
             smem,
-            pl.BlockSpec((SEG, model), lambda s: (s, 0)),
+            pl.BlockSpec((per * SEG, model), lambda s: (s, 0)),
             pl.BlockSpec(weights.shape, lambda s: (0, 0)),
         ],
         out_specs=[
-            pl.BlockSpec((SEG, heads * dim), lambda s: (s, 0)),
-            pl.BlockSpec((SEG, heads * dim), lambda s: (s, 0)),
-            pl.BlockSpec((1, heads, dim, dim), lambda s: (s, 0, 0, 0)),
-            pl.BlockSpec((1, heads, dim, dim), lambda s: (s, 0, 0, 0)),
+            pl.BlockSpec((per * SEG, heads * dim), lambda s: (s, 0)),
+            pl.BlockSpec((per * SEG, heads * dim), lambda s: (s, 0)),
+            pl.BlockSpec((per, heads, dim, dim), lambda s: (s, 0, 0, 0)),
+            pl.BlockSpec((per, heads, dim, dim), lambda s: (s, 0, 0, 0)),
         ],
         out_shape=[flat, flat, maps, maps],
-        compiler_params=pltpu.CompilerParams(vmem_limit_bytes=40 * MIB),
+        compiler_params=pltpu.CompilerParams(vmem_limit_bytes=48 * MIB),
     )(own_lengths, decay_rate, tokens, weights)
 
 
@@ -358,67 +378,190 @@
     own_lengths = lax.dynamic_slice_in_dim(lengths, first_seg, local_count, 0)
     weights = jnp.concatenate(
         [
-            lin_qkv.reshape(model_width, -1),
-            lin_gates.reshape(model_width, -1),
+            lin_qkv[:, 0],
+            lin_qkv[:, 1],
+            lin_qkv[:, 2],
+            lin_gates[:, 0],
+            lin_gates[:, 1],
             jnp.zeros((model_width, 128 - 2 * local_heads), bf16),
         ],
         axis=1,
     )
+    kv_head = tensor_idx // (tensor_count // KV_HEADS)
+    own_kv = jnp.concatenate(
+        [
+            lax.dynamic_slice_in_dim(att_kv[:, c], kv_head * att_dim, att_dim, 1)
+            for c in range(2)
+        ],
+        axis=1,
+    )
+    seg_ids = jnp.arange(segment_count)
+    parent_map = ((parents[:, None] == seg_ids[None, :]) & (seg_ids[:, None] > 0)).astype(f32)
+    seen = (ancestor_table(parent_map) > 0.5) | (seg_ids[:, None] == seg_ids[None, :])
+    seen = lax.dynamic_slice_in_dim(seen, first_seg, local_count, 0)
+    places = jnp.arange(SEG)
+    key_valid = places[None, :] < lengths[:, None]
+    bias = jnp.where(seen[:, :, None] & key_valid[None], 0.0, -1e30)
+    bias = bias.astype(f32).reshape(local_count, segment_count * SEG)
+    valid = (places[None, :] < own_lengths[:, None]).astype(f32).reshape(local_rows, 1)
     o1, q2, amap, bmap = delta_terms(tokens, weights, own_lengths, decay_rate, head_dim)
     lin_mixed, normed = mix_rows(
         parents, amap, bmap, o1, q2, full_out, tokens, norm_gain[None, :]
     )
-    return attend(lin_mixed, normed, parents, lengths, att_q, att_kv)
-
-
-def attend(lin_mixed, normed, parents, lengths, att_q, att_kv):
-    branch_idx = lax.axis_index("branch")
-    tensor_count = lax.axis_size("tensor")
-    tensor_idx = lax.axis_index("tensor")
-    local_rows, model_width = normed.shape
-    local_count = local_rows // SEG
-    segment_count = lax.axis_size("branch") * local_count
-    first_seg = branch_idx * local_count
-    att_dim = ATT_DIM
-    seg_ids = jnp.arange(segment_count)
-    local_flag = seg_ids[None, :] == (first_seg + jnp.arange(local_count))[:, None]
-    own_lengths = jnp.sum(jnp.where(local_flag, lengths[None, :], 0), axis=1)
-    valid = (jnp.arange(SEG)[None, :] < own_lengths[:, None]).reshape(local_rows)
-    row_local = jnp.arange(local_rows)
-    query_seg = first_seg + row_local // SEG
-    query_pos = row_local % SEG
-    parent_map = ((parents[:, None] == seg_ids[None, :]) & (seg_ids[:, None] > 0)).astype(f32)
-    ancestry = ancestor_table(parent_map)
-    local_anc = (jnp.dot(local_flag.astype(f32), ancestry, precision=highest) > 0.5).astype(f32)
-    query_anc = jnp.repeat(local_anc, SEG, axis=0)
-    local_q = att_q.shape[1] // att_dim
-    kv_head = tensor_idx // (tensor_count // KV_HEADS)
-    scale_factor = 1.0 / math.sqrt(att_dim)
-    own_kv = lax.dynamic_slice_in_dim(att_kv, kv_head * att_dim, att_dim, 2)
-    kv = jnp.dot(normed, own_kv.reshape(model_width, -1), preferred_element_type=f32).astype(bf16)
-    full_kv = lax.all_gather(kv, "branch", axis=0, tiled=True)
-    key_part, value_part = full_kv[:, :att_dim], full_kv[:, att_dim:]
-    queries = jnp.dot(normed, att_q, preferred_element_type=f32).astype(bf16)
-    queries = queries.reshape(local_rows, local_q, att_dim)
-    global_rows = jnp.arange(key_part.shape[0])
-    key_seg = global_rows // SEG
-    key_pos = global_rows % SEG
-    match = key_seg[:, None] == seg_ids[None, :]
-    key_limit = jnp.sum(jnp.where(match, lengths[None, :], 0), axis=1)
-    key_ancestor = jnp.dot(query_anc, match.astype(f32).T, precision=highest) > 0.5
-    own_branch = (key_seg[None, :] == query_seg[:, None]) & (key_pos[None, :] <= query_pos[:, None])
-    allowed = (key_pos < key_limit)[None, :] & (key_ancestor | own_branch)
-    scores = (
-        jnp.einsum("qhd,kd->hqk", queries, key_part, preferred_element_type=f32) * scale_factor
-    )
-    top = jnp.max(jnp.where(allowed[None], scores, -1e30), axis=-1)
-    numer = jnp.where(allowed[None], jnp.exp(scores - top[..., None]), 0.0)
-    sums = jnp.sum(numer, axis=-1)
-    accum = jnp.einsum("hqk,kd->hqd", numer.astype(bf16), value_part, preferred_element_type=f32)
-    result = accum / sums[..., None]
-    result = jnp.swapaxes(result, 0, 1).reshape(local_rows, local_q * att_dim)
-    att_out = jnp.where(valid[:, None], result, 0.0).astype(bf16)
-    return (lin_mixed, att_out)
+    return lin_mixed, attend(normed, att_q, own_kv, bias, valid)
+
+
+def attend_kernel(
+    branches, tensors, normed_ref, q_w_ref, kv_w_ref, bias_ref, valid_ref, out_ref,
+    kv, queries, accum, top, sums, far_send, far_recv, pass_send, pass_recv,
+):
+    me_b = lax.axis_index("branch")
+    me_t = lax.axis_index("tensor")
+    core = lax.rem(me_t, 2)
+    partner = me_t + 1 - 2 * core
+    rows = normed_ref.shape[0]
+    count = rows // SEG
+    half = rows // 2
+    heads = q_w_ref.shape[1] // ATT_DIM
+
+    barrier = pltpu.get_barrier_semaphore()
+    for d in range(1, branches):
+        pl.semaphore_signal(
+            barrier, inc=1, device_id={"branch": lax.rem(me_b + d, branches)}, device_id_type=MESH
+        )
+    pl.semaphore_signal(barrier, inc=1, device_id={"tensor": partner}, device_id_type=MESH)
+
+    def keys_of(branch, part):
+        return pl.ds(pl.multiple_of(branch * rows + part * half, half), half)
+
+    def far_copy(peer, source):
+        return pltpu.make_async_remote_copy(
+            src_ref=kv.at[keys_of(source, core)], dst_ref=kv.at[keys_of(source, core)],
+            send_sem=far_send.at[peer], recv_sem=far_recv.at[source],
+            device_id={"branch": peer}, device_id_type=MESH,
+        )
+
+    def pass_copy(source, part):
+        return pltpu.make_async_remote_copy(
+            src_ref=kv.at[keys_of(source, part)], dst_ref=kv.at[keys_of(source, part)],
+            send_sem=pass_send.at[source], recv_sem=pass_recv.at[source],
+            device_id={"tensor": partner}, device_id_type=MESH,
+        )
+
+    def project_half(part):
+        at = pl.ds(pl.multiple_of(part * half, half), half)
+        kv[keys_of(me_b, part), :] = dot1(normed_ref[at, :], kv_w_ref[...]).astype(bf16)
+
+    project_half(core)
+    pl.semaphore_wait(barrier, branches)
+    for peer in range(1, branches):
+        @pl.when(me_b < peer)
+        def _():
+            far_copy(peer, me_b).start()
+    project_half(1 - core)
+
+    scale = 1.0 / math.sqrt(ATT_DIM)
+
+    def query_rows(j):
+        return pl.ds(pl.multiple_of(j * SEG, SEG), SEG)
+
+    def project(j, carry):
+        part = dot1(normed_ref[query_rows(j), :], q_w_ref[...]).astype(bf16) * scale
+        for h in range(heads):
+            queries[j, h * SEG : (h + 1) * SEG, :] = (
+                part[:, h * ATT_DIM : (h + 1) * ATT_DIM].astype(bf16)
+            )
+        return carry
+
+    lax.fori_loop(0, count, project, 0)
+
+    causal_row = lax.broadcasted_iota(jnp.int32, (heads * SEG, SEG), 0) % SEG
+    causal_col = lax.broadcasted_iota(jnp.int32, (heads * SEG, SEG), 1)
+    causal = jnp.where(causal_col <= causal_row, 0.0, -1e30)
+    for j in range(count):
+        seen = j + 1
+        span = pl.ds(pl.multiple_of(me_b * rows, SEG), seen * SEG)
+        scores = dot1(queries[j], kv[span, :ATT_DIM], NT) + bias_ref[j : j + 1, span]
+        tail = scores[:, j * SEG :] + causal
+        scores = tail if j == 0 else jnp.concatenate([scores[:, : j * SEG], tail], axis=1)
+        best = jnp.max(scores, axis=1, keepdims=True)
+        numer = jnp.exp(scores - best)
+        top[j] = jnp.broadcast_to(best, top.shape[1:])
+        sums[j] = jnp.broadcast_to(jnp.sum(numer, axis=1, keepdims=True), sums.shape[1:])
+        accum[j] = dot1(numer.astype(bf16), kv[span, ATT_DIM:])
+
+    def earlier(source, carry):
+        far_copy(0, source).wait_recv()
+        pass_copy(source, core).start()
+        pass_copy(source, 1 - core).wait_recv()
+        span = pl.ds(pl.multiple_of(source * rows, SEG), rows)
+
+        def one(j, inner):
+            scores = dot1(queries[j], kv[span, :ATT_DIM], NT) + bias_ref[pl.ds(j, 1), span]
+            old = top[j][:, :1]
+            best = jnp.maximum(old, jnp.max(scores, axis=1, keepdims=True))
+            numer = jnp.exp(scores - best)
+            keep = jnp.exp(old - best)
+            top[j] = jnp.broadcast_to(best, top.shape[1:])
+            sums[j] = sums[j] * keep + jnp.sum(numer, axis=1, keepdims=True)
+            accum[j] = accum[j] * keep + dot1(numer.astype(bf16), kv[span, ATT_DIM:])
+            return inner
+
+        lax.fori_loop(0, count, one, 0)
+        return carry
+
+    lax.fori_loop(0, me_b, earlier, 0)
+
+    def store(j, carry):
+        result = accum[j] / sums[j][:, :1]
+        keep = valid_ref[query_rows(j), :] > 0
+        for h in range(heads):
+            out_ref[query_rows(j), h * ATT_DIM : (h + 1) * ATT_DIM] = jnp.where(
+                keep, result[h * SEG : (h + 1) * SEG], 0.0
+            ).astype(bf16)
+        return carry
+
+    lax.fori_loop(0, count, store, 0)
+
+    for peer in range(1, branches):
+        @pl.when(me_b < peer)
+        def _():
+            far_copy(peer, me_b).wait_send()
+
+    def finish(source, carry):
+        pass_copy(source, core).wait_send()
+        return carry
+
+    lax.fori_loop(0, me_b, finish, 0)
+
+
+def attend(normed, att_q, own_kv, bias, valid):
+    branches, tensors = lax.axis_size("branch"), lax.axis_size("tensor")
+    rows = normed.shape[0]
+    count = rows // SEG
+    heads = att_q.shape[1] // ATT_DIM
+    vmem = pl.BlockSpec(memory_space=pltpu.VMEM)
+    dma = pltpu.SemaphoreType.DMA
+    return pl.pallas_call(
+        functools.partial(attend_kernel, branches, tensors),
+        in_specs=[vmem] * 5,
+        out_specs=vmem,
+        out_shape=jax.ShapeDtypeStruct((rows, att_q.shape[1]), bf16),
+        scratch_shapes=[
+            pltpu.VMEM((branches * rows, 2 * ATT_DIM), bf16),
+            pltpu.VMEM((count, heads * SEG, ATT_DIM), bf16),
+            pltpu.VMEM((count, heads * SEG, ATT_DIM), f32),
+            pltpu.VMEM((count, heads * SEG, 128), f32),
+            pltpu.VMEM((count, heads * SEG, 128), f32),
+            dma((branches,)),
+            dma((branches,)),
+            dma((branches,)),
+            dma((branches,)),
+        ],
+        compiler_params=pltpu.CompilerParams(
+            collective_id=1, has_side_effects=True, vmem_limit_bytes=56 * MIB
+        ),
+    )(normed, att_q, own_kv, bias, valid)
 
 
 def solution(mesh):

time: 174 us -> 141 us (0.81); the launches traced: 171 us -> 141 us
  matrix products: 37.4 us -> 1.44 us
  Pallas kernels: 69.4 us -> 86.7 us
  waiting for transfers between devices: 15.8 us -> 0.68 us
  local copies, waits for them, and re-layouts: 29.6 us -> 35.6 us
  other arithmetic: 4.57 us -> 2.36 us
    dot_general x5 -> x0, matrix products: 23.5 us -> none  [the longest x1 6.95 us: attend(): jnp.einsum('hqk,kd->hqd', numer.astype(bf16), value_part, preferred_eleme...]
    pallas_call x1 -> x2, Pallas kernels: 33.3 us -> 50.6 us  [the longest x1 28.3 us: attend(): pl.pallas_call(functools.partial(attend_kernel, branches, tensors), in_sp...]
    all_gather x1 -> x0, waiting for transfers between devices: 15.1 us -> none  [attend(): full_kv = lax.all_gather(kv, 'branch', axis=0, tiled=True)]
    sub x1 -> x0, matrix products: 12.5 us -> none  [attend(): numer = jnp.where(allowed[None], jnp.exp(scores - top[..., None]), 0.0)]
    slice x0 -> x2, local copies, waits for them, and re-layouts: none -> 9.26 us  [the longest x1 9.24 us: on_device(): att_kv[:, c]]
    reshape x4 -> x0, local copies, waits for them, and re-layouts: 7.26 us -> none  [the longest x1 4.67 us: on_device(): lin_qkv.reshape(model_width, -1)]
    concatenate x1, local copies, waits for them, and re-layouts: 0.08 us -> 6.68 us  [on_device(): jnp.concatenate([lin_qkv[:, 0], lin_qkv[:, 1], lin_qkv[:, 2], lin_gates[:...]
    and x1 -> x0, local copies, waits for them, and re-layouts: 6.07 us -> none  [attend(): allowed = (key_pos < key_limit)[None, :] & (key_ancestor | own_branch)]
  transfers between devices with their start and end apart: 2 -> 1, of which waited for: 1 -> 0; matrix products, arithmetic and copies ran while one was open for 22% -> 23% of each run, Pallas kernels for 19% -> 16%
where the time goes in v2:
time: 141 us
  Pallas kernels  86.7 us (61%)
  local copies, waits for them, and re-layouts  35.6 us (25%)
  between operations  14.2 us (10%)
  other arithmetic  2.36 us (2%)
  matrix products  1.44 us (1%)
    pallas_call x1, Pallas kernels, mix_rows(): pl.pallas_call(functools.partial(mix_kernel, branches, tensors), in_specs...  36.2 us
    pallas_call x1, Pallas kernels, attend(): pl.pallas_call(functools.partial(attend_kernel, branches, tensors), in_sp...  28.3 us
    pallas_call x1, Pallas kernels, delta_terms(): pl.pallas_call(functools.partial(delta_kernel, heads, dim, per), grid=(co...  22.2 us
    unnamed x30, local copies, waits for them, and re-layouts  10.9 us
    slice x1, local copies, waits for them, and re-layouts, on_device(): att_kv[:, c]  9.24 us
    concatenate x1, local copies, waits for them, and re-layouts, on_device(): jnp.concatenate([lin_qkv[:, 0], lin_qkv[:, 1], lin_qkv[:, 2], lin_gates[:...  6.68 us
    dynamic_slice x1, local copies, waits for them, and re-layouts, on_device(): lax.dynamic_slice_in_dim(att_kv[:, c], kv_head * att_dim, att_dim, 1)  4.39 us
    squeeze x1, local copies, waits for them, and re-layouts, on_device(): lin_qkv[:, 2]  3.38 us
  transfers between devices with their start and end apart: 1, of which 0 were waited for; matrix products, arithmetic and copies ran while one was open for 23% of the time, Pallas kernels for 16%

profile of v2, /device:TPU:11, one launch (start us, length us, event | category | flops | bytes accessed | tf_op | source)
XLA Modules:
  0.0 141.1 jit_solution(10271115392835957799)
XLA Ops:
  7.2 0.0 all-gather.2.cloned.1.call-start
  7.2 0.7 all-gather.2.cloned.1.call-update
  7.9 9.2 %fusion.10 = (bf16[2048,1,512]{2,1,0:T(2,128)(2,1)S(1)}, bf16[2048,1,512]{2,1,0:T(2,128)(2,1)S(1)}) fusion(bf16[2048,2,512]{2,1,0:T(2,128)(2,1)} %param.21), kind=kLoop, calls=%fused_computation.27 | loop fusion | bytes 8388608 | tf_op jit(solution)/shard_map/slice | solution.py:393
  17.2 4.4 %constant_dynamic-slice_fusion.1 = (bf16[2048,1,256]{2,1,0:T(2,128)(2,1)S(1)}, bf16[2048,1,256]{2,1,0:T(2,128)(2,1)S(1)}) fusion(bf16[2048,1,512]{2,1,0:T(2,128)(2,1)S(1)} %get-tuple-element.53, s32[]{:T(128)S(6)} %select_n.20, bf16[2048,1,512]{2,1,0:T(2,128)(2,1)S(1)} %get-tuple-element.52), kind=kLoop, calls=%fused_computation.24 | loop fusion | bytes 4194308 | tf_op jit(solution)/shard_map/dynamic_slice | solution.py:393
  21.6 0.0 copy-start.6
  21.6 0.0 copy-start.8
  21.6 0.0 copy-start.7
  21.6 0.2 copy.31
  21.8 0.2 copy.32
  22.0 0.3 copy-done.6
  22.3 1.1 copy.19
  23.4 1.1 copy.20
  24.5 0.0 copy-done.8
  24.5 0.1 dynamic_slice.16.lens_ref
  24.6 0.0 copy-done.7
  24.6 0.1 fusion.8
  24.7 1.5 %while.11 = (s32[]{:T(128)}, f32[8,8]{1,0:T(8,128)S(1)}, s32[8]{0:T(128)S(1)}, pred[8]{0:T(512)(128)(4,1)S(1)}, s32[]{:T(128)}) while((s32[]{:T(128)}, f32[8,8]{1,0:T(8,128)S(1)}, s32[8]{0:T(128)S(1)}, pred[8]{0:T(512)(128)(4,1)S(1)}, s32[]{:T(128)}) %tuple.37), condition=%wide.region_1.2_spmd.clone, body=%wide.region_0.1_spmd.clone.sunk | while | flops 6402 | bytes 1125 | solution.py:53
  24.7 0.2 convolution_add_fusion.2
  24.9 0.2 convolution_add_fusion.2
  25.1 0.2 convolution_add_fusion.2
  25.3 0.2 convolution_add_fusion.2
  25.5 0.2 convolution_add_fusion.2
  25.7 0.2 convolution_add_fusion.2
  25.9 0.2 convolution_add_fusion.2
  26.2 0.1 broadcast_bitcast_fusion
  26.3 0.1 convert_bitcast_fusion
  26.4 1.0 copy.28
  27.4 0.1 lt.57
  27.5 3.4 %slice_bitcast_fusion = (bf16[2048,256]{1,0:T(8,128)(2,1)S(1)}, bf16[2048,256]{1,0:T(8,128)(2,1)}, bf16[2048,256]{1,0:T(8,128)(2,1)}) fusion(bf16[2048,3,256]{2,0,1:T(8,128)(2,1)} %param.15), kind=kLoop, calls=%fused_computation.10 | loop fusion | bytes 6291456 | tf_op jit(solution)/shard_map/squeeze | solution.py:383
  30.9 0.9 broadcast_in_dim.10
  31.8 0.0 copy-start.4
  31.8 6.7 %concatenate.6.w_ref = bf16[2048,896]{1,0:T(8,128)(2,1)} concatenate(bf16[2048,256]{1,0:T(8,128)(2,1)} %get-tuple-element.55, bf16[2048,256]{1,0:T(8,128)(2,1)} %get-tuple-element.56, bf16[2048,256]{1,0:T(8,128)(2,1)S(1)} %get-tuple-element.54, bf16[2048,2]{1,0:T(8,128)(2,1)} %bitcast.32, bf16[2048,2]{1,0:T(8,128)(2,1)} %bitcast.33, bf16[2048,124]{1,0:T(8,128)(2,1)} %broadcast_in_dim.10), dimensions={1} | concatenate | bytes 7340032 | tf_op jit(solution)/shard_map/concatenate | solution.py:379
  38.5 0.0 copy-done.4
  38.5 22.2 %shard_map.113 = (f32[1024,256]{1,0:T(8,128)S(1)}, f32[1024,256]{1,0:T(8,128)S(1)}, f32[4,2,128,128]{3,2,1,0:T(8,128)S(1)}, f32[4,2,128,128]{3,2,1,0:T(8,128)S(1)}) custom-call(s32[4]{0:T(128)S(1)} %dynamic_slice.16.lens_ref, f32[2]{0:T(128)S(1)} %copy-done.4, bf16[1024,2048]{1,0:T(8,128)(2,1)} %tok_ref.3, bf16[2048,896]{1,0:T(8,128)(2,1)} %concatenate.6.w_ref), custom_call_target="tpu_custom_call" | custom-call | tf_op jit(solution)/shard_map/pallas_call | solution.py:140
  60.7 0.0 copy-start
  60.7 1.0 copy-done
  61.7 0.0 copy-start.1
  61.7 1.0 copy-done.1
  62.6 0.0 copy-start.2
  62.6 0.8 copy-done.2
  63.5 0.0 copy-start.3
  63.5 0.8 copy-done.3
  64.3 1.6 %pad_maximum_fusion.kv_w_ref = bf16[2048,512]{1,0:T(8,128)(2,1)} fusion(bf16[2048,256]{1,0:T(8,128)(2,1)S(1)} %bitcast.30, bf16[2048,256]{1,0:T(8,128)(2,1)S(1)} %bitcast.31), kind=kLoop, calls=%fused_computation.7 | loop fusion | flops 4194304 | bytes 4194304 | tf_op jit(solution)/shard_map/concatenate | solution.py:391
  65.8 0.6 and_select_fusion.bias_ref
  66.5 0.0 all-gather.2.cloned.1.call-done.lin_out_ref
  66.5 36.2 %shard_map.114 = (bf16[256,2048]{1,0:T(8,128)(2,1)}, bf16[1024,2048]{1,0:T(8,128)(2,1)}) custom-call(s32[8]{0:T(128)S(1)} %get-tuple-element.109, f32[4,2,128,128]{3,2,1,0:T(8,128)} %copy-done.2, f32[4,2,128,128]{3,2,1,0:T(8,128)} %copy-done.3, f32[1024,256]{1,0:T(8,128)} %copy-done, f32[1024,256]{1,0:T(8,128)} %copy-done.1, ...), custom_call_target="tpu_custom_call" | custom-call | tf_op jit(solution)/shard_map/pallas_call | solution.py:335
  102.7 0.0 copy-start.5
  102.7 28.3 %shard_map.115 = bf16[1024,512]{1,0:T(8,128)(2,1)} custom-call(bf16[1024,2048]{1,0:T(8,128)(2,1)} %get-tuple-element.30.normed_ref, bf16[2048,512]{1,0:T(8,128)(2,1)} %q_w_ref.1, bf16[2048,512]{1,0:T(8,128)(2,1)} %pad_maximum_fusion.kv_w_ref, f32[4,2048]{1,0:T(4,128)} %and_select_fusion.bias_ref, f32[1024,1]{1,0:T(8,128)} %bitcast.34), custom_call_target="tpu_custom_call" | custom-call | tf_op jit(solution)/shard_map/pallas_call | solution.py:545
  131.0 0.0 copy-done.5
  131.0 1.0 copy.44
  132.0 2.3 %copy.45 = bf16[1024,512]{1,0:T(8,128)(2,1)} copy(bf16[1024,512]{1,0:T(8,128)(2,1)} %shard_map.115) | data formatting | bytes 2097152
  (16 shorter events, 0.1 us)
Async XLA Ops:
  7.2 59.3 %all-gather.2.cloned.1.call-start = ((), (), s32[]{:S(2)}) async-start(), calls=%async_computation | async-start | bytes 5242880 | tf_op jit(solution)/shard_map/all_gather | solution.py:377
  21.6 0.7 copy-start.6
  21.6 2.9 %copy-start.8 = (s32[8]{0:T(128)S(1)}, s32[8]{0:T(128)}, u32[]{:S(2)}) copy-start(s32[8]{0:T(128)} %param.14) | copy-start | bytes 100
  21.6 3.0 %copy-start.7 = (s32[8]{0:T(128)S(1)}, s32[8]{0:T(128)}, u32[]{:S(2)}) copy-start(s32[8]{0:T(128)} %parents_ref.1) | copy-start | bytes 100
  31.8 6.7 %copy-start.4 = (f32[2]{0:T(128)S(1)}, f32[2]{0:T(128)}, u32[]{:S(2)}) copy-start(f32[2]{0:T(128)} %rate_ref.1) | copy-start | bytes 28
  60.7 1.0 copy-start
  61.7 1.0 copy-start.1
  62.6 0.8 copy-start.2
  63.5 0.8 copy-start.3
  102.7 28.3 %copy-start.5 = (bf16[256,2048]{1,0:T(8,128)(2,1)S(1)}, bf16[256,2048]{1,0:T(8,128)(2,1)}, u32[]{:S(2)}) copy-start(bf16[256,2048]{1,0:T(8,128)(2,1)} %get-tuple-element.103) | copy-start | bytes 3145732
Sparse Core Ops, SparseCore 0:
  9.6 36.0 all-gather.1

commit v3 on v2

--- a/solution.py
+++ b/solution.py
@@ -44,19 +44,12 @@
     return matrix * lax.rsqrt(jnp.sum(matrix * matrix, axis=-1, keepdims=True) + 1e-06)
 
 
-def ancestor_table(parent_map):
-    count = parent_map.shape[0]
-
-    def widen(counter, table):
-        return parent_map + jnp.dot(parent_map, table, precision=highest)
-
-    return lax.fori_loop(0, count - 1, widen, parent_map)
-
-
 def delta_kernel(
-    heads, dim, per, lens_ref, rate_ref, tok_ref, w_ref, o1_ref, q2_ref, a_ref, b_ref
+    heads, dim, per, lens_ref, rate_ref, tok_ref, w_ref, gate_ref, o1_ref, q2_ref, a_ref, b_ref
 ):
-    proj_all = dot1(tok_ref[...], w_ref[...])
+    toks = tok_ref[...]
+    projected = [dot1(toks, w_ref[c]) for c in range(3)]
+    gates_all = dot1(toks, gate_ref[...], NT)
     half = SEG // 2
     rows = lax.broadcasted_iota(jnp.int32, (SEG, SEG), 0)
     cols = lax.broadcasted_iota(jnp.int32, (SEG, SEG), 1)
@@ -66,18 +59,19 @@
     hrows = lax.broadcasted_iota(jnp.int32, (half, half), 0)
     hcols = lax.broadcasted_iota(jnp.int32, (half, half), 1)
     places = lax.broadcasted_iota(jnp.int32, (SEG, 1), 0)
-    width = heads * dim
     eye = (hrows == hcols).astype(f32)
     parts = []
     for g in range(per):
         valid = places < lens_ref[pl.program_id(0) * per + g]
-        proj = proj_all[g * SEG : (g + 1) * SEG]
+        queries, keys, values = (p[g * SEG : (g + 1) * SEG] for p in projected)
+        gates = gates_all[g * SEG : (g + 1) * SEG]
         for h in range(heads):
-            q = unit_rows(proj[:, h * dim : (h + 1) * dim]) / math.sqrt(dim)
-            k = unit_rows(proj[:, width + h * dim : width + (h + 1) * dim])
-            v = proj[:, 2 * width + h * dim : 2 * width + (h + 1) * dim]
-            g0 = proj[:, 3 * width + h : 3 * width + h + 1]
-            g1 = proj[:, 3 * width + heads + h : 3 * width + heads + h + 1]
+            at = slice(h * dim, (h + 1) * dim)
+            q = unit_rows(queries[:, at]) / math.sqrt(dim)
+            k = unit_rows(keys[:, at])
+            v = values[:, at]
+            g0 = gates[:, h : h + 1]
+            g1 = gates[:, heads + h : heads + h + 1]
             beta = jnp.where(valid, 1.0 / (1.0 + jnp.exp(-g1)), 0.0)
             soft = jnp.maximum(g0, 0.0) + jnp.log1p(jnp.exp(-jnp.abs(g0)))
             step = jnp.where(valid, -rate_ref[h] * soft, 0.0)
@@ -129,7 +123,7 @@
             a_ref[g, h] = overall * eye - ends[:, dim:]
 
 
-def delta_terms(tokens, weights, own_lengths, decay_rate, dim):
+def delta_terms(tokens, weights, gates, own_lengths, decay_rate, dim):
     heads = decay_rate.shape[0]
     rows, model = tokens.shape
     count = rows // SEG
@@ -144,7 +138,8 @@
             smem,
             smem,
             pl.BlockSpec((per * SEG, model), lambda s: (s, 0)),
-            pl.BlockSpec(weights.shape, lambda s: (0, 0)),
+            pl.BlockSpec(weights.shape, lambda s: (0, 0, 0)),
+            pl.BlockSpec(gates.shape, lambda s: (0, 0)),
         ],
         out_specs=[
             pl.BlockSpec((per * SEG, heads * dim), lambda s: (s, 0)),
@@ -154,7 +149,7 @@
         ],
         out_shape=[flat, flat, maps, maps],
         compiler_params=pltpu.CompilerParams(vmem_limit_bytes=48 * MIB),
-    )(own_lengths, decay_rate, tokens, weights)
+    )(own_lengths, decay_rate, tokens, weights, gates)
 
 
 def mix_kernel(
@@ -376,43 +371,31 @@
     first_seg = branch_idx * local_count
     full_out = lax.all_gather(lin_out, "tensor", axis=0, tiled=True)
     own_lengths = lax.dynamic_slice_in_dim(lengths, first_seg, local_count, 0)
-    weights = jnp.concatenate(
-        [
-            lin_qkv[:, 0],
-            lin_qkv[:, 1],
-            lin_qkv[:, 2],
-            lin_gates[:, 0],
-            lin_gates[:, 1],
-            jnp.zeros((model_width, 128 - 2 * local_heads), bf16),
-        ],
-        axis=1,
-    )
+    weights = jnp.transpose(lin_qkv, (1, 0, 2))
+    gates = jnp.transpose(lin_gates, (1, 2, 0)).reshape(2 * local_heads, model_width)
     kv_head = tensor_idx // (tensor_count // KV_HEADS)
-    own_kv = jnp.concatenate(
-        [
-            lax.dynamic_slice_in_dim(att_kv[:, c], kv_head * att_dim, att_dim, 1)
-            for c in range(2)
-        ],
-        axis=1,
-    )
+    own_kv = lax.dynamic_slice_in_dim(att_kv, kv_head * att_dim, att_dim, 2)
+    own_kv = own_kv.reshape(model_width, 2 * att_dim)
     seg_ids = jnp.arange(segment_count)
     parent_map = ((parents[:, None] == seg_ids[None, :]) & (seg_ids[:, None] > 0)).astype(f32)
-    seen = (ancestor_table(parent_map) > 0.5) | (seg_ids[:, None] == seg_ids[None, :])
+    reach = parent_map + jnp.eye(segment_count, dtype=f32)
+    for _ in range((segment_count - 1).bit_length()):
+        reach = (jnp.dot(reach, reach, precision=highest) > 0.5).astype(f32)
+    seen = reach > 0.5
     seen = lax.dynamic_slice_in_dim(seen, first_seg, local_count, 0)
     places = jnp.arange(SEG)
     key_valid = places[None, :] < lengths[:, None]
     bias = jnp.where(seen[:, :, None] & key_valid[None], 0.0, -1e30)
     bias = bias.astype(f32).reshape(local_count, segment_count * SEG)
-    valid = (places[None, :] < own_lengths[:, None]).astype(f32).reshape(local_rows, 1)
-    o1, q2, amap, bmap = delta_terms(tokens, weights, own_lengths, decay_rate, head_dim)
+    o1, q2, amap, bmap = delta_terms(tokens, weights, gates, own_lengths, decay_rate, head_dim)
     lin_mixed, normed = mix_rows(
         parents, amap, bmap, o1, q2, full_out, tokens, norm_gain[None, :]
     )
-    return lin_mixed, attend(normed, att_q, own_kv, bias, valid)
+    return lin_mixed, attend(normed, att_q, own_kv, bias, own_lengths)
 
 
 def attend_kernel(
-    branches, tensors, normed_ref, q_w_ref, kv_w_ref, bias_ref, valid_ref, out_ref,
+    branches, tensors, normed_ref, q_w_ref, kv_w_ref, bias_ref, lens_ref, out_ref,
     kv, queries, accum, top, sums, far_send, far_recv, pass_send, pass_recv,
 ):
     me_b = lax.axis_index("branch")
@@ -514,7 +497,7 @@
 
     def store(j, carry):
         result = accum[j] / sums[j][:, :1]
-        keep = valid_ref[query_rows(j), :] > 0
+        keep = lax.broadcasted_iota(jnp.int32, (SEG, 1), 0) < lens_ref[j]
         for h in range(heads):
             out_ref[query_rows(j), h * ATT_DIM : (h + 1) * ATT_DIM] = jnp.where(
                 keep, result[h * SEG : (h + 1) * SEG], 0.0
@@ -535,7 +518,7 @@
     lax.fori_loop(0, me_b, finish, 0)
 
 
-def attend(normed, att_q, own_kv, bias, valid):
+def attend(normed, att_q, own_kv, bias, own_lengths):
     branches, tensors = lax.axis_size("branch"), lax.axis_size("tensor")
     rows = normed.shape[0]
     count = rows // SEG
@@ -544,7 +527,7 @@
     dma = pltpu.SemaphoreType.DMA
     return pl.pallas_call(
         functools.partial(attend_kernel, branches, tensors),
-        in_specs=[vmem] * 5,
+        in_specs=[vmem] * 4 + [pl.BlockSpec(memory_space=pltpu.SMEM)],
         out_specs=vmem,
         out_shape=jax.ShapeDtypeStruct((rows, att_q.shape[1]), bf16),
         scratch_shapes=[
@@ -561,7 +544,7 @@
         compiler_params=pltpu.CompilerParams(
             collective_id=1, has_side_effects=True, vmem_limit_bytes=56 * MIB
         ),
-    )(normed, att_q, own_kv, bias, valid)
+    )(normed, att_q, own_kv, bias, own_lengths)
 
 
 def solution(mesh):

time: 141 us -> 119 us (0.84)
  local copies, waits for them, and re-layouts: 35.6 us -> 12.9 us
  waiting for transfers between devices: 0.68 us -> 5.45 us
  other arithmetic: 2.36 us -> 0.63 us
    slice x2 -> x0, local copies, waits for them, and re-layouts: 9.26 us -> none  [the longest x1 9.24 us: on_device(): att_kv[:, c]]
    concatenate x1 -> x0, local copies, waits for them, and re-layouts: 6.68 us -> none  [on_device(): jnp.concatenate([lin_qkv[:, 0], lin_qkv[:, 1], lin_qkv[:, 2], lin_gates[:...]
    all_gather x1, waiting for transfers between devices: 0.01 us -> 4.77 us  [on_device(): full_out = lax.all_gather(lin_out, 'tensor', axis=0, tiled=True)]
    squeeze x1 -> x0, local copies, waits for them, and re-layouts: 3.38 us -> none  [on_device(): lin_qkv[:, 2]]
    unnamed x30 -> x25, local copies, waits for them, and re-layouts: 10.9 us -> 8.78 us
    concatenate x1 -> x0, other arithmetic: 1.56 us -> none  [on_device(): jnp.concatenate([lax.dynamic_slice_in_dim(att_kv[:, c], kv_head * att_dim...]
  transfers between devices with their start and end apart: 1 -> 1, of which waited for: 0 -> 1; matrix products, arithmetic and copies ran while one was open for 23% -> 6% of each run, Pallas kernels for 16% -> 19%
where the time goes in v3:
time: 119 us
  Pallas kernels  85.3 us (72%)
  between operations  14.2 us (12%)
  local copies, waits for them, and re-layouts  12.9 us (11%)
  waiting for transfers between devices  5.45 us (5%)
    pallas_call x1, Pallas kernels, mix_rows(): pl.pallas_call(functools.partial(mix_kernel, branches, tensors), in_specs...  35.1 us
    pallas_call x1, Pallas kernels, attend(): pl.pallas_call(functools.partial(attend_kernel, branches, tensors), in_sp...  28.2 us
    pallas_call x1, Pallas kernels, delta_terms(): pl.pallas_call(functools.partial(delta_kernel, heads, dim, per), grid=(co...  22.1 us
    unnamed x25, local copies, waits for them, and re-layouts  8.78 us
    all_gather x1, waiting for transfers between devices, on_device(): full_out = lax.all_gather(lin_out, 'tensor', axis=0, tiled=True)  4.77 us
    dynamic_slice x1, local copies, waits for them, and re-layouts, on_device(): own_kv = lax.dynamic_slice_in_dim(att_kv, kv_head * att_dim, att_dim, 2)  3.25 us
  transfers between devices with their start and end apart: 1, of which 1 were waited for; matrix products, arithmetic and copies ran while one was open for 6% of the time, Pallas kernels for 19%

profile of v3, /device:TPU:11, one launch (start us, length us, event | category | flops | bytes accessed | tf_op | source)
XLA Modules:
  0.0 119.0 jit_solution(17233268296116616572)
XLA Ops:
  7.2 0.0 all-gather.2.cloned.1.call-start
  7.2 0.7 all-gather.2.cloned.1.call-update
  7.9 0.7 reshape.38.gate_ref
  8.7 0.0 copy-start.8
  8.7 0.0 copy-start.7
  8.7 0.0 copy-start.5
  8.7 3.3 %constant_dynamic-slice_fusion.1 = bf16[2048,2,256]{2,1,0:T(2,128)(2,1)S(1)} fusion(bf16[2048,2,512]{2,1,0:T(2,128)(2,1)} %param.19, s32[]{:T(128)S(6)} %select_n.19), kind=kLoop, calls=%fused_computation.18 | loop fusion | bytes 4194308 | tf_op jit(solution)/shard_map/dynamic_slice | solution.py:377
  12.0 1.9 %copy.12 = bf16[256,8,2,256]{3,1,2,0:T(8,128)(2,1)} copy(bf16[256,8,2,256]{3,2,1,0:T(2,128)(2,1)S(1)} %bitcast.17) | data formatting | bytes 4194304
  13.8 0.0 copy-done.8
  13.8 0.1 dynamic_slice.9.lens_ref
  13.9 0.0 copy-start.4
  13.9 0.0 copy-done.7
  13.9 0.2 convolution_compare_fusion
  14.1 0.1 convolution_compare_fusion.2
  14.2 0.1 fusion.1
  14.4 0.1 broadcast_bitcast_fusion
  14.5 0.1 lt.32
  14.6 0.0 copy-done.5
  14.6 22.1 %shard_map.113 = (f32[1024,256]{1,0:T(8,128)S(1)}, f32[1024,256]{1,0:T(8,128)S(1)}, f32[4,2,128,128]{3,2,1,0:T(8,128)S(1)}, f32[4,2,128,128]{3,2,1,0:T(8,128)S(1)}) custom-call(s32[4]{0:T(128)S(1)} %dynamic_slice.9.lens_ref, f32[2]{0:T(128)S(1)} %copy-done.5, bf16[1024,2048]{1,0:T(8,128)(2,1)} %tok_ref.3, bf16[3,2048,256]{2,1,0:T(8,128)(2,1)} %bitcast.18, ...), custom_call_target="tpu_custom_call" | custom-call | tf_op jit(solution)/shard_map/pallas_call | solution.py:134
  36.7 0.0 copy-start
  36.7 1.0 copy-done
  37.7 0.0 copy-start.1
  37.7 1.0 copy-done.1
  38.6 0.0 copy-start.2
  38.6 0.8 copy-done.2
  39.4 0.0 copy-start.3
  39.4 0.8 copy-done.3
  40.2 0.6 and_select_fusion.bias_ref
  40.9 4.8 %all-gather.2.cloned.1.call-done.lin_out_ref = bf16[1024,2048]{1,0:T(8,128)(2,1)} async-done(((bf16[256,2048]{1,0:T(8,128)(2,1)}), bf16[1024,2048]{1,0:T(8,128)(2,1)}) %all-gather.2.cloned.1.call-update) | async-done | bytes 4194320 | tf_op jit(solution)/shard_map/all_gather | solution.py:372
  45.6 35.1 %shard_map.114 = (bf16[256,2048]{1,0:T(8,128)(2,1)}, bf16[1024,2048]{1,0:T(8,128)(2,1)}) custom-call(s32[8]{0:T(128)} %parents_ref.1, f32[4,2,128,128]{3,2,1,0:T(8,128)} %copy-done.2, f32[4,2,128,128]{3,2,1,0:T(8,128)} %copy-done.3, f32[1024,256]{1,0:T(8,128)} %copy-done, f32[1024,256]{1,0:T(8,128)} %copy-done.1, ...), custom_call_target="tpu_custom_call" | custom-call | tf_op jit(solution)/shard_map/pallas_call | solution.py:330
  80.7 0.0 copy-done.4
  80.7 0.0 copy-start.6
  80.7 28.2 %shard_map.115 = bf16[1024,512]{1,0:T(8,128)(2,1)} custom-call(bf16[1024,2048]{1,0:T(8,128)(2,1)} %get-tuple-element.13.normed_ref, bf16[2048,512]{1,0:T(8,128)(2,1)} %q_w_ref.1, bf16[2048,512]{1,0:T(8,128)(2,1)} %bitcast.16, f32[4,2048]{1,0:T(4,128)} %and_select_fusion.bias_ref, s32[4]{0:T(128)} %copy-done.4), custom_call_target="tpu_custom_call" | custom-call | tf_op jit(solution)/shard_map/pallas_call | solution.py:528
  108.9 0.0 copy-done.6
  108.9 1.0 copy.17
  109.9 2.3 %copy.18 = bf16[1024,512]{1,0:T(8,128)(2,1)} copy(bf16[1024,512]{1,0:T(8,128)(2,1)} %shard_map.115) | data formatting | bytes 2097152
  (6 shorter events, 0.1 us)
Async XLA Ops:
  7.2 38.5 %all-gather.2.cloned.1.call-start = ((), (), s32[]{:S(2)}) async-start(), calls=%async_computation | async-start | bytes 5242880 | tf_op jit(solution)/shard_map/all_gather | solution.py:372
  8.7 5.2 %copy-start.8 = (s32[8]{0:T(128)S(1)}, s32[8]{0:T(128)}, u32[]{:S(2)}) copy-start(s32[8]{0:T(128)} %param.12) | copy-start | bytes 100
  8.7 5.3 %copy-start.7 = (s32[8]{0:T(128)S(1)}, s32[8]{0:T(128)}, u32[]{:S(2)}) copy-start(s32[8]{0:T(128)} %parents_ref.1) | copy-start | bytes 100
  8.7 5.9 %copy-start.5 = (f32[2]{0:T(128)S(1)}, f32[2]{0:T(128)}, u32[]{:S(2)}) copy-start(f32[2]{0:T(128)} %rate_ref.1) | copy-start | bytes 28
  13.9 66.8 %copy-start.4 = (s32[4]{0:T(128)}, s32[4]{0:T(128)S(1)}, u32[]{:S(2)}) copy-start(s32[4]{0:T(128)S(1)} %dynamic_slice.9.lens_ref) | copy-start | bytes 52
  36.7 1.0 copy-start
  37.7 1.0 copy-start.1
  38.6 0.8 copy-start.2
  39.4 0.8 copy-start.3
  80.7 28.2 %copy-start.6 = (bf16[256,2048]{1,0:T(8,128)(2,1)S(1)}, bf16[256,2048]{1,0:T(8,128)(2,1)}, u32[]{:S(2)}) copy-start(bf16[256,2048]{1,0:T(8,128)(2,1)} %get-tuple-element.16) | copy-start | bytes 3145732
Sparse Core Ops, SparseCore 0:
  9.6 36.0 all-gather.1

commit v4 on v3

--- a/solution.py
+++ b/solution.py
@@ -148,7 +148,7 @@
             pl.BlockSpec((per, heads, dim, dim), lambda s: (s, 0, 0, 0)),
         ],
         out_shape=[flat, flat, maps, maps],
-        compiler_params=pltpu.CompilerParams(vmem_limit_bytes=48 * MIB),
+        compiler_params=pltpu.CompilerParams(vmem_limit_bytes=36 * MIB),
     )(own_lengths, decay_rate, tokens, weights, gates)
 
 
@@ -351,7 +351,7 @@
             dma((chunks, fars)),
         ],
         compiler_params=pltpu.CompilerParams(
-            collective_id=0, has_side_effects=True, vmem_limit_bytes=56 * MIB
+            collective_id=0, has_side_effects=True, vmem_limit_bytes=30 * MIB
         ),
     )(parents, amap, bmap, o1, q2, lin_out, tokens, gain)
 
@@ -542,7 +542,7 @@
             dma((branches,)),
         ],
         compiler_params=pltpu.CompilerParams(
-            collective_id=1, has_side_effects=True, vmem_limit_bytes=56 * MIB
+            collective_id=1, has_side_effects=True, vmem_limit_bytes=30 * MIB
         ),
     )(normed, att_q, own_kv, bias, own_lengths)
 

time: 119 us -> 116 us (0.975)
  Pallas kernels: 85.3 us -> 73.2 us
  local copies, waits for them, and re-layouts: 12.9 us -> 21.1 us
    unnamed x25 -> x37, local copies, waits for them, and re-layouts: 8.78 us -> 17 us
    pallas_call x1, Pallas kernels: 35.1 us -> 29 us  [mix_rows(): pl.pallas_call(functools.partial(mix_kernel, branches, tensors), in_specs...]
    pallas_call x1, Pallas kernels: 28.2 us -> 24.2 us  [attend(): pl.pallas_call(functools.partial(attend_kernel, branches, tensors), in_sp...]
    pallas_call x1, Pallas kernels: 22.1 us -> 20 us  [delta_terms(): pl.pallas_call(functools.partial(delta_kernel, heads, dim, per), grid=(co...]
  transfers between devices with their start and end apart: 1 -> 1, of which waited for: 1 -> 1; matrix products, arithmetic and copies ran while one was open for 6% -> 5% of each run, Pallas kernels for 19% -> 17%
where the time goes in v4:
time: 116 us; the launch traced here: 115 us
  Pallas kernels  73.2 us (63%)
  local copies, waits for them, and re-layouts  21.1 us (18%)
  between operations  14.2 us (12%)
  waiting for transfers between devices  6.27 us (5%)
    pallas_call x1, Pallas kernels, mix_rows(): pl.pallas_call(functools.partial(mix_kernel, branches, tensors), in_specs...  29 us
    pallas_call x1, Pallas kernels, attend(): pl.pallas_call(functools.partial(attend_kernel, branches, tensors), in_sp...  24.2 us
    pallas_call x1, Pallas kernels, delta_terms(): pl.pallas_call(functools.partial(delta_kernel, heads, dim, per), grid=(co...  20 us
    unnamed x37, local copies, waits for them, and re-layouts  17 us
    all_gather x1, waiting for transfers between devices, on_device(): full_out = lax.all_gather(lin_out, 'tensor', axis=0, tiled=True)  5.59 us
    dynamic_slice x1, local copies, waits for them, and re-layouts, on_device(): own_kv = lax.dynamic_slice_in_dim(att_kv, kv_head * att_dim, att_dim, 2)  3.25 us
  transfers between devices with their start and end apart: 1, of which 1 were waited for; matrix products, arithmetic and copies ran while one was open for 5% of the time, Pallas kernels for 17%

profile of v4, /device:TPU:11, one launch (start us, length us, event | category | flops | bytes accessed | tf_op | source)
XLA Modules:
  0.0 115.3 jit_solution(3822776909924161574)
XLA Ops:
  7.2 0.0 all-gather.2.cloned.1.call-start
  7.2 0.7 all-gather.2.cloned.1.call-update
  7.9 0.7 reshape.38.gate_ref
  8.7 0.0 copy-start.14
  8.7 0.0 copy-start.13
  8.7 0.0 copy-start.12
  8.7 3.3 %constant_dynamic-slice_fusion.1 = bf16[2048,2,256]{2,1,0:T(2,128)(2,1)S(1)} fusion(bf16[2048,2,512]{2,1,0:T(2,128)(2,1)} %param.19, s32[]{:T(128)S(6)} %select_n.19), kind=kLoop, calls=%fused_computation.18 | loop fusion | bytes 4194308 | tf_op jit(solution)/shard_map/dynamic_slice | solution.py:377
  12.0 0.5 copy.12
  12.5 0.0 copy-start.11
  12.5 0.0 copy-done.14
  12.5 0.1 dynamic_slice.9.lens_ref
  12.6 0.0 copy-done.13
  12.6 0.2 convolution_compare_fusion
  12.8 0.1 convolution_compare_fusion.2
  12.9 0.1 fusion.1
  13.1 0.1 broadcast_bitcast_fusion
  13.2 0.1 lt.32
  13.3 0.0 copy-done.12
  13.3 0.0 copy-start
  13.3 2.2 %copy-done = bf16[1024,2048]{1,0:T(8,128)(2,1)S(1)} copy-done((bf16[1024,2048]{1,0:T(8,128)(2,1)S(1)}, bf16[1024,2048]{1,0:T(8,128)(2,1)}, u32[]{:S(2)}) %copy-start) | copy-done | bytes 4194328
  15.5 0.0 copy-start.3
  15.5 1.9 %copy-done.3 = bf16[2048,3,256]{2,0,1:T(8,128)(2,1)S(1)} copy-done((bf16[2048,3,256]{2,0,1:T(8,128)(2,1)S(1)}, bf16[2048,3,256]{2,0,1:T(8,128)(2,1)}, u32[]{:S(2)}) %copy-start.3) | copy-done | bytes 3145752
  17.4 20.0 %shard_map.113 = (f32[1024,256]{1,0:T(8,128)S(1)}, f32[1024,256]{1,0:T(8,128)S(1)}, f32[4,2,128,128]{3,2,1,0:T(8,128)S(1)}, f32[4,2,128,128]{3,2,1,0:T(8,128)S(1)}) custom-call(s32[4]{0:T(128)S(1)} %dynamic_slice.9.lens_ref, f32[2]{0:T(128)S(1)} %copy-done.12, bf16[1024,2048]{1,0:T(8,128)(2,1)S(1)} %copy-done, bf16[3,2048,256]{2,1,0:T(8,128)(2,1)S(1)} %bitcast.17, ...), custom_call_target="tpu_custom_call" | custom-call | tf_op jit(solution)/shard_map/pallas_call | solution.py:134
  37.5 0.0 copy-start.5
  37.5 1.0 copy-done.5
  38.4 0.0 copy-start.7
  38.4 0.8 copy-done.7
  39.2 0.0 copy-start.9
  39.2 0.8 copy-done.9
  40.0 5.6 %all-gather.2.cloned.1.call-done.lin_out_ref = bf16[1024,2048]{1,0:T(8,128)(2,1)} async-done(((bf16[256,2048]{1,0:T(8,128)(2,1)}), bf16[1024,2048]{1,0:T(8,128)(2,1)}) %all-gather.2.cloned.1.call-update) | async-done | bytes 4194320 | tf_op jit(solution)/shard_map/all_gather | solution.py:372
  45.6 0.0 copy-done.11
  45.6 0.0 copy-start.1
  45.6 2.2 %copy-done.1 = bf16[1024,2048]{1,0:T(8,128)(2,1)S(1)} copy-done((bf16[1024,2048]{1,0:T(8,128)(2,1)S(1)}, bf16[1024,2048]{1,0:T(8,128)(2,1)}, u32[]{:S(2)}) %copy-start.1) | copy-done | bytes 4194328
  47.8 0.0 copy-start.2
  47.8 2.2 %copy-done.2 = bf16[1024,2048]{1,0:T(8,128)(2,1)S(1)} copy-done((bf16[1024,2048]{1,0:T(8,128)(2,1)S(1)}, bf16[1024,2048]{1,0:T(8,128)(2,1)}, u32[]{:S(2)}) %copy-start.2) | copy-done | bytes 4194328
  50.0 0.0 copy-start.6
  50.0 1.2 %copy-done.6 = f32[1024,256]{1,0:T(8,128)S(1)} copy-done((f32[1024,256]{1,0:T(8,128)S(1)}, f32[1024,256]{1,0:T(8,128)}, u32[]{:S(2)}) %copy-start.6) | copy-done | bytes 1048600
  51.2 0.0 copy-start.8
  51.2 1.0 copy-done.8
  52.3 0.0 copy-start.10
  52.3 1.0 copy-done.10
  53.3 0.0 copy-start.4
  53.3 29.0 %shard_map.114 = (bf16[256,2048]{1,0:T(8,128)(2,1)S(1)}, bf16[1024,2048]{1,0:T(8,128)(2,1)S(1)}) custom-call(s32[8]{0:T(128)S(1)} %copy-done.13, f32[4,2,128,128]{3,2,1,0:T(8,128)S(1)} %copy-done.8, f32[4,2,128,128]{3,2,1,0:T(8,128)S(1)} %copy-done.10, f32[1024,256]{1,0:T(8,128)S(1)} %get-tuple-element.10.o1_ref, f32[1024,256]{1,0:T(8,128)S(1)} %copy-done.6, ...), custom_call_target="tpu_custom_call" | custom-call | tf_op jit(solution)/shard_map/pallas_call | solution.py:330
  82.3 0.0 copy-done.4
  82.3 24.2 %shard_map.115 = bf16[1024,512]{1,0:T(8,128)(2,1)S(1)} custom-call(bf16[1024,2048]{1,0:T(8,128)(2,1)S(1)} %get-tuple-element.13.normed_ref, bf16[2048,512]{1,0:T(8,128)(2,1)S(1)} %copy-done.4, bf16[2048,512]{1,0:T(8,128)(2,1)S(1)} %bitcast.16, f32[4,2048]{1,0:T(4,128)S(1)} %and_select_fusion.bias_ref, s32[4]{0:T(128)S(1)} %dynamic_slice.9.lens_ref), custom_call_target="tpu_custom_call" | custom-call | tf_op jit(solution)/shard_map/pallas_call | solution.py:528
  106.5 1.0 copy.17
  107.5 1.0 copy.18
  (7 shorter events, 0.1 us)
Async XLA Ops:
  7.2 38.5 %all-gather.2.cloned.1.call-start = ((), (), s32[]{:S(2)}) async-start(), calls=%async_computation | async-start | bytes 5242880 | tf_op jit(solution)/shard_map/all_gather | solution.py:372
  8.7 3.8 %copy-start.14 = (s32[8]{0:T(128)S(1)}, s32[8]{0:T(128)}, u32[]{:S(2)}) copy-start(s32[8]{0:T(128)} %param.12) | copy-start | bytes 100
  8.7 3.9 %copy-start.13 = (s32[8]{0:T(128)S(1)}, s32[8]{0:T(128)}, u32[]{:S(2)}) copy-start(s32[8]{0:T(128)} %parents_ref.1) | copy-start | bytes 100
  8.7 4.6 %copy-start.12 = (f32[2]{0:T(128)S(1)}, f32[2]{0:T(128)}, u32[]{:S(2)}) copy-start(f32[2]{0:T(128)} %rate_ref.1) | copy-start | bytes 28
  12.5 33.1 %copy-start.11 = (f32[2048]{0:T(1024)S(1)}, f32[2048]{0:T(1024)}, u32[]{:S(2)}) copy-start(f32[2048]{0:T(1024)} %param.17) | copy-start | bytes 24580
  13.3 2.2 %copy-start = (bf16[1024,2048]{1,0:T(8,128)(2,1)S(1)}, bf16[1024,2048]{1,0:T(8,128)(2,1)}, u32[]{:S(2)}) copy-start(bf16[1024,2048]{1,0:T(8,128)(2,1)} %tok_ref.3) | copy-start | bytes 12582916
  15.5 1.9 %copy-start.3 = (bf16[2048,3,256]{2,0,1:T(8,128)(2,1)S(1)}, bf16[2048,3,256]{2,0,1:T(8,128)(2,1)}, u32[]{:S(2)}) copy-start(bf16[2048,3,256]{2,0,1:T(8,128)(2,1)} %param.13) | copy-start | bytes 9437188
  37.5 1.0 copy-start.5
  38.4 0.8 copy-start.7
  39.2 0.8 copy-start.9
  45.6 2.2 %copy-start.1 = (bf16[1024,2048]{1,0:T(8,128)(2,1)S(1)}, bf16[1024,2048]{1,0:T(8,128)(2,1)}, u32[]{:S(2)}) copy-start(bf16[1024,2048]{1,0:T(8,128)(2,1)} %tok_ref.3) | copy-start | bytes 12582916
  47.8 2.2 %copy-start.2 = (bf16[1024,2048]{1,0:T(8,128)(2,1)S(1)}, bf16[1024,2048]{1,0:T(8,128)(2,1)}, u32[]{:S(2)}) copy-start(bf16[1024,2048]{1,0:T(8,128)(2,1)} %all-gather.2.cloned.1.call-done.lin_out_ref) | copy-start | bytes 12582916
  50.0 1.2 %copy-start.6 = (f32[1024,256]{1,0:T(8,128)S(1)}, f32[1024,256]{1,0:T(8,128)}, u32[]{:S(2)}) copy-start(f32[1024,256]{1,0:T(8,128)} %copy-done.5) | copy-start | bytes 3145732
  51.2 1.0 copy-start.8
  52.3 1.0 copy-start.10
  53.3 29.0 %copy-start.4 = (bf16[2048,512]{1,0:T(8,128)(2,1)S(1)}, bf16[2048,512]{1,0:T(8,128)(2,1)}, u32[]{:S(2)}) copy-start(bf16[2048,512]{1,0:T(8,128)(2,1)} %q_w_ref.1) | copy-start | bytes 6291460
Sparse Core Ops, SparseCore 0:
  9.6 36.0 all-gather.1
